TPU v7x, 32 devices: a whole 2x2x4 slice. The times are simulated.
32 devices in a mesh: groups: 2 (over y), shot: 4 (over z), depth: 2 (over x), freq: 2 (over core).
Axes of the slice: x: 2, y: 2, z: 4, core: 2. Of those that a mesh axis runs over, the one named last changes fastest.
Arguments:
- source: float32 [8, 6, 2, 256, 256], P(('groups', 'shot'), 'freq'), parts along dimension 0, may hold values from -6 to 6
- receiver: float32 [8, 6, 2, 256, 256], P(('groups', 'shot'), 'freq'), parts along dimension 0, may hold values from -6 to 6
- slowness: float32 [8, 4, 256, 256], P(('groups', 'shot'), 'depth'), parts along dimension 0, may hold values from 0.6 to 1.4
- omegas: float32 [8, 6], P(('groups', 'shot'), 'freq'), parts along dimension 0, may hold values from 0.5 to 2.5
- shot_start: int32 [8], P(('groups', 'shot')), parts along dimension 0, may hold values from 0 to 256, as said below
Outputs:
- image: float32 [1024, 4, 256], P(('groups', 'shot'), 'depth', 'freq'), parts along dimension 0
There are 2 independent parts, one for each index of `groups`. A program takes and returns all parts, laid end to end along the dimension named above; each array names one. Nothing has to cross between parts.
Inputs may be any that keep to these rules, and one draw needn't show every extreme that they name: `shot_start`: any shot group's aperture may begin at any column of the survey. Shot group 4 // 2 begins at column 0 and shot group 0 at 256.
All inputs are finite; a program needn't handle non-finite values.
Results may differ from a plain program's by a relative error of at most 0.03.
Values may be sent and summed in bfloat16 or wider, within the bound.
A program may use at most 64 MiB of HBM per device.

v0:
```python
import jax
import jax.numpy as jnp
from jax import lax
from jax.sharding import PartitionSpec as P

TILE = 128


def from_behind(array, axis, by):
    peers = lax.axis_size(axis)
    pairs = [(i, i + by) for i in range(peers) if 0 <= i + by < peers]
    return lax.ppermute(array, axis, pairs)


def tables(points):
    positions = jnp.arange(points, dtype=jnp.int32)
    product = positions[:, None] * positions[None, :] % points
    angles = 2.0 * jnp.pi / points * product.astype(jnp.float32)
    cosine_table = jnp.cos(angles).astype(jnp.bfloat16)
    sine_table = jnp.sin(angles).astype(jnp.bfloat16)
    forward = jnp.concatenate(
        [
            jnp.concatenate([cosine_table, -sine_table], axis=1),
            jnp.concatenate([sine_table, cosine_table], axis=1),
        ],
        axis=0,
    )
    inverse = jnp.concatenate(
        [
            jnp.concatenate([cosine_table, sine_table], axis=1),
            jnp.concatenate([-sine_table, cosine_table], axis=1),
        ],
        axis=0,
    )
    return (forward, inverse)


def lateral_grids(points):
    positions = jnp.arange(points, dtype=jnp.int32)
    wrapped = (positions + points // 2) % points - points // 2
    wavenumber = 2.0 * jnp.pi / points * wrapped.astype(jnp.float32)
    edge_width = points // 16
    distance_in = jnp.minimum(positions, points - 1 - positions) + 1
    edge_taper = jnp.minimum(distance_in.astype(jnp.float32) / edge_width, 1.0)
    return (wavenumber, edge_taper)


def flip_parts(field_in):
    leading = field_in.shape[:-2]
    row_count = field_in.shape[-2]
    col_count = field_in.shape[-1] // 2
    pieces = field_in.reshape(leading + (row_count, 2, col_count))
    moved = jnp.swapaxes(pieces, -3, -1)
    return moved.reshape(leading + (col_count, 2 * row_count))


def extrapolate(
    wave_state, slow_level, angular, field_signs, forward, inverse, wavenumber, edge_taper
):
    batch_size, points, width = wave_state.shape
    inv_points = 1.0 / points
    half_done = jnp.dot(
        wave_state.reshape(batch_size * points, width), forward, preferred_element_type=jnp.float32
    )
    half_done = flip_parts(half_done.astype(jnp.bfloat16).reshape(batch_size, points, width))
    spectrum = jnp.dot(
        half_done.reshape(batch_size * points, width), forward, preferred_element_type=jnp.float32
    ).reshape(batch_size, points, width)
    mean_slow = jnp.mean(slow_level)
    radius_sq = jnp.square(angular * mean_slow)
    square = jnp.square(wavenumber)[:, None] + jnp.square(wavenumber)[None, :]
    vertical = radius_sq[:, None, None] - square[None]
    real_kz = jnp.sqrt(jnp.maximum(vertical, 0.0))
    damping = jnp.exp(-jnp.sqrt(jnp.maximum(-vertical, 0.0)))
    phase_turn = field_signs[:, None, None] * real_kz
    phase_real = damping * jnp.cos(phase_turn)
    phase_imag = damping * jnp.sin(phase_turn)
    spec_real = spectrum[..., :points]
    spec_imag = spectrum[..., points:]
    shifted = jnp.concatenate(
        [
            spec_real * phase_real - spec_imag * phase_imag,
            spec_real * phase_imag + spec_imag * phase_real,
        ],
        axis=-1,
    ).astype(jnp.bfloat16)
    half_back = (
        jnp.dot(
            shifted.reshape(batch_size * points, width), inverse, preferred_element_type=jnp.float32
        )
        * inv_points
    )
    half_back = flip_parts(half_back.astype(jnp.bfloat16).reshape(batch_size, points, width))
    field_out = (
        jnp.dot(
            half_back.reshape(batch_size * points, width),
            inverse,
            preferred_element_type=jnp.float32,
        ).reshape(batch_size, points, width)
        * inv_points
    )
    correction = (field_signs * angular)[:, None, None] * (slow_level - mean_slow)[None]
    window = edge_taper[:, None] * edge_taper[None, :]
    corr_real = jnp.cos(correction) * window[None]
    corr_imag = jnp.sin(correction) * window[None]
    field_real = field_out[..., :points]
    field_imag = field_out[..., points:]
    return (
        field_real * corr_real - field_imag * corr_imag,
        field_real * corr_imag + field_imag * corr_real,
    )


def local(source, receiver, slowness, omegas, shot_start):
    points = source.shape[-1]
    fronts = source.shape[1]
    levels = slowness.shape[1]
    segments = lax.axis_size("depth")
    segment_index = lax.axis_index("depth")
    forward, inverse = tables(points)
    wavenumber, edge_taper = lateral_grids(points)
    field_signs = jnp.array([-1.0, 1.0], jnp.float32)

    def surface(chosen):
        src_front = lax.dynamic_index_in_dim(source[0], chosen, 0, keepdims=False)
        rcv_front = lax.dynamic_index_in_dim(receiver[0], chosen, 0, keepdims=False)
        paired = jnp.stack([src_front, rcv_front])
        return jnp.concatenate([paired[:, 0], paired[:, 1]], axis=-1).astype(jnp.bfloat16)

    def extrapolate_front(operands):
        wave_state, rate_now = operands
        angular = jnp.stack([rate_now, rate_now])
        level_terms = []
        for level_index in range(levels):
            real_part, imag_part = extrapolate(
                wave_state,
                slowness[0, level_index],
                angular,
                field_signs,
                forward,
                inverse,
                wavenumber,
                edge_taper,
            )
            level_terms.append(real_part[0] * real_part[1] + imag_part[0] * imag_part[1])
            wave_state = jnp.concatenate([real_part, imag_part], axis=-1).astype(jnp.bfloat16)
        return (wave_state, jnp.stack(level_terms, axis=1))

    def stay_still(operands):
        wave_state, rate_now = operands
        return (jnp.zeros_like(wave_state), jnp.zeros((points, levels, points), jnp.float32))

    def one_turn(turn_index, carry):
        incoming, image_sum = carry
        front_index = turn_index - segment_index
        active = jnp.logical_and(front_index >= 0, front_index < fronts)
        chosen = jnp.clip(front_index, 0, fronts - 1)
        begin_field = jnp.where(segment_index == 0, surface(chosen), incoming)
        rate_now = lax.dynamic_index_in_dim(omegas[0], chosen, 0, keepdims=False)
        wave_state, level_image = lax.cond(
            active, extrapolate_front, stay_still, (begin_field, rate_now)
        )
        incoming = from_behind(wave_state, "depth", 1)
        return (incoming, image_sum + level_image)

    initial = (
        jnp.zeros((2, points, 2 * points), jnp.bfloat16),
        jnp.zeros((points, levels, points), jnp.float32),
    )
    final_carry = lax.fori_loop(0, segments + fronts - 1, one_turn, initial)
    local_image = lax.psum_scatter(
        final_carry[1].astype(jnp.bfloat16), "freq", scatter_dimension=2, tiled=True
    ).astype(jnp.float32)
    aperture_start = shot_start[0]
    owners = lax.axis_size("shot")
    survey_cols = owners * TILE
    padding = jnp.zeros((survey_cols,) + local_image.shape[1:], jnp.float32)
    padded = jnp.concatenate([padding, local_image, padding], axis=0)
    offset = jnp.clip(
        jnp.zeros((), jnp.int32) - aperture_start + survey_cols, 0, points + survey_cols
    )
    placed = lax.dynamic_slice_in_dim(padded, offset, survey_cols, 0)
    blocks = placed.reshape((owners, TILE) + local_image.shape[1:])
    received = lax.all_to_all(
        blocks.astype(jnp.bfloat16), "shot", split_axis=0, concat_axis=0, tiled=True
    ).astype(blocks.dtype)
    collected = jnp.sum(received, axis=0)
    return collected


def solution(mesh):
    return jax.shard_map(
        local,
        mesh=mesh,
        in_specs=(
            P(("groups", "shot"), "freq", None, None, None),
            P(("groups", "shot"), "freq", None, None, None),
            P(("groups", "shot"), "depth", None, None),
            P(("groups", "shot"), "freq"),
            P(("groups", "shot")),
        ),
        out_specs=P(("groups", "shot"), "depth", "freq"),
        check_vma=False,
    )
```

profile of v0, /device:TPU:2, one launch (start us, length us, event | category | flops | bytes accessed | tf_op | source)
XLA Modules:
  0.0 210.5 jit_solution(7978232508442241251)
XLA Ops:
  8.7 2.4 %convert.56 = bf16[1,3,2,256,256]{4,3,2,1,0:T(8,128)(2,1)} convert(f32[1,3,2,256,256]{4,3,2,1,0:T(8,128)} %param.10) | non-fusion elementwise | flops 393216 | bytes 2359296
  13.1 163.9 %while.19 = (s32[]{:T(128)}, bf16[2,256,512]{2,1,0:T(8,128)(2,1)S(1)}, f32[256,2,256]{2,0,1:T(8,128)}, s32[]{:T(128)}, bf16[1,3,2,256,256]{4,3,2,1,0:T(8,128)(2,...) while((s32[]{:T(128)}, ...), condition=%wide.region_5.6_spmd.clone.clone.clone, body=%wide.region_0.5_spmd.sunk.clone.clone.clone.sunk | while | flops 2163611136 | bytes 54534728 | solution.py:170
  17.4 35.3 %collective-permute-done = bf16[2,256,512]{2,1,0:T(8,128)(2,1)S(1)} collective-permute-done((bf16[2,256,512]{2,1,0:T(8,128)(2,1)}, bf16[2,256,512]{2,1,0:T(8,128)(2,1)S(1)}, u32[]{:S(2)}, u32[]{:S(2)}) %collective-permute-start) | collective-permute-done | bytes 524320 | tf_op jit(solution)/shard_map/while/body/eval_jaxpr/ppermute | solution.py:12
  53.9 25.3 %conditional.6 = (bf16[2,256,512]{2,1,0:T(8,128)(2,1)}, f32[256,2,256]{2,0,1:T(8,128)S(1)}) conditional(s32[]{:T(128)} %convert_element_type.155, () %tuple.108, (pred[]{:T(512)}, bf16[2,256,512]{2,1,0:T(8,128)(2,1)S(1)}, bf16[2,256,512]{2,1,0:T(8,128)(2,1)S(1)}, bf16[512,512]{1,0:T(8,128)(2,1)S(1)}, f32[1,3]{1,0:T(1,128)S(1)}, ...), branch_computations={%region_1.1_spmd, %region_2.4_spmd.clone} | conditional | flops 2162033664 | bytes 46668028 | solution.py:160
  59.7 2.7 %subtract_convert_fusion.1 = (bf16[2,256,256]{2,1,0:T(8,128)(2,1)S(1)}, bf16[2,256,256]{2,1,0:T(8,128)(2,1)S(1)}) fusion(f32[2,256,512]{2,1,0:T(8,128)S(1)} %fusion.55, f32[2]{0:T(128)S(1)} %copy-done.3, f32[256,256]{1,0:T(8,128)S(1)} %broadcast_add_fusion, f32[2]{0:T(128)S(1)} %get-tuple-element.564), kind=kLoop, calls=%fused_computation.74 | loop fusion | flops 2097152 | bytes 1835024 | tf_op jit(solution)/shard_map/convert.13
  66.2 2.1 %fusion.86 = (bf16[2,256,256]{2,1,0:T(8,128)(2,1)S(1)}, f32[2,256,256]{2,1,0:T(8,128)S(1)}, bf16[2,256,256]{2,1,0:T(8,128)(2,1)S(1)}, f32[2,256,256]{2,1,0:T(8,128)S(1)}) fusion(f32[2,256,512]{2,1,0:T(8,128)S(1)} %convolution_multiply_fusion.2, f32[256,256]{1,0:T(8,128)S(1)} %broadcast_multiply_fusion, f32[256,256]{1,0:T(8,128)S(1)} %get-tuple-element.560, ...), kind=kLoop, calls=%fused_computation.143 | loop fusion | flops 1441792 | bytes 3145736 | tf_op jit(solution)/shard_map/convert.9
  70.8 2.7 %subtract_convert_fusion = (bf16[2,256,256]{2,1,0:T(8,128)(2,1)S(1)}, bf16[2,256,256]{2,1,0:T(8,128)(2,1)S(1)}) fusion(f32[2,256,512]{2,1,0:T(8,128)S(1)} %fusion.53, f32[2]{0:T(128)S(1)} %get-tuple-element.563, f32[2]{0:T(128)S(1)} %copy-done.3, f32[256,256]{1,0:T(8,128)S(1)} %broadcast_add_fusion), kind=kLoop, calls=%fused_computation.72 | loop fusion | flops 2097152 | bytes 1835024 | tf_op jit(solution)/shard_map/convert.5
  76.1 2.1 %fusion.82 = (bf16[2,256,256]{2,1,0:T(8,128)(2,1)S(1)}, f32[2,256,256]{2,1,0:T(8,128)S(1)}, bf16[2,256,256]{2,1,0:T(8,128)(2,1)S(1)}, f32[2,256,256]{2,1,0:T(8,128)S(1)}) fusion(f32[2,256,512]{2,1,0:T(8,128)S(1)} %convolution_multiply_fusion, f32[256,256]{1,0:T(8,128)S(1)} %broadcast_multiply_fusion, f32[256,256]{1,0:T(8,128)S(1)} %copy-done.1, f32[2]{0:T(128)S(1)} %fusion.64), kind=kLoop, calls=%fused_computation.141 | loop fusion | flops 1441792 | bytes 3145736 | tf_op jit(solution)/shard_map/convert
  80.5 1.9 select_add_fusion.2
  82.4 12.6 %collective-permute-done = bf16[2,256,512]{2,1,0:T(8,128)(2,1)S(1)} collective-permute-done((bf16[2,256,512]{2,1,0:T(8,128)(2,1)}, bf16[2,256,512]{2,1,0:T(8,128)(2,1)S(1)}, u32[]{:S(2)}, u32[]{:S(2)}) %collective-permute-start) | collective-permute-done | bytes 524320 | tf_op jit(solution)/shard_map/while/body/eval_jaxpr/ppermute | solution.py:12
  96.2 25.3 %conditional.6 = (bf16[2,256,512]{2,1,0:T(8,128)(2,1)}, f32[256,2,256]{2,0,1:T(8,128)S(1)}) conditional(s32[]{:T(128)} %convert_element_type.155, () %tuple.108, (pred[]{:T(512)}, bf16[2,256,512]{2,1,0:T(8,128)(2,1)S(1)}, bf16[2,256,512]{2,1,0:T(8,128)(2,1)S(1)}, bf16[512,512]{1,0:T(8,128)(2,1)S(1)}, f32[1,3]{1,0:T(1,128)S(1)}, ...), branch_computations={%region_1.1_spmd, %region_2.4_spmd.clone} | conditional | flops 2162033664 | bytes 46668028 | solution.py:160
  102.0 2.7 %subtract_convert_fusion.1 = (bf16[2,256,256]{2,1,0:T(8,128)(2,1)S(1)}, bf16[2,256,256]{2,1,0:T(8,128)(2,1)S(1)}) fusion(f32[2,256,512]{2,1,0:T(8,128)S(1)} %fusion.55, f32[2]{0:T(128)S(1)} %copy-done.3, f32[256,256]{1,0:T(8,128)S(1)} %broadcast_add_fusion, f32[2]{0:T(128)S(1)} %get-tuple-element.564), kind=kLoop, calls=%fused_computation.74 | loop fusion | flops 2097152 | bytes 1835024 | tf_op jit(solution)/shard_map/convert.13
  108.6 2.1 %fusion.86 = (bf16[2,256,256]{2,1,0:T(8,128)(2,1)S(1)}, f32[2,256,256]{2,1,0:T(8,128)S(1)}, bf16[2,256,256]{2,1,0:T(8,128)(2,1)S(1)}, f32[2,256,256]{2,1,0:T(8,128)S(1)}) fusion(f32[2,256,512]{2,1,0:T(8,128)S(1)} %convolution_multiply_fusion.2, f32[256,256]{1,0:T(8,128)S(1)} %broadcast_multiply_fusion, f32[256,256]{1,0:T(8,128)S(1)} %get-tuple-element.560, ...), kind=kLoop, calls=%fused_computation.143 | loop fusion | flops 1441792 | bytes 3145736 | tf_op jit(solution)/shard_map/convert.9
  113.1 2.7 %subtract_convert_fusion = (bf16[2,256,256]{2,1,0:T(8,128)(2,1)S(1)}, bf16[2,256,256]{2,1,0:T(8,128)(2,1)S(1)}) fusion(f32[2,256,512]{2,1,0:T(8,128)S(1)} %fusion.53, f32[2]{0:T(128)S(1)} %get-tuple-element.563, f32[2]{0:T(128)S(1)} %copy-done.3, f32[256,256]{1,0:T(8,128)S(1)} %broadcast_add_fusion), kind=kLoop, calls=%fused_computation.72 | loop fusion | flops 2097152 | bytes 1835024 | tf_op jit(solution)/shard_map/convert.5
  118.4 2.1 %fusion.82 = (bf16[2,256,256]{2,1,0:T(8,128)(2,1)S(1)}, f32[2,256,256]{2,1,0:T(8,128)S(1)}, bf16[2,256,256]{2,1,0:T(8,128)(2,1)S(1)}, f32[2,256,256]{2,1,0:T(8,128)S(1)}) fusion(f32[2,256,512]{2,1,0:T(8,128)S(1)} %convolution_multiply_fusion, f32[256,256]{1,0:T(8,128)S(1)} %broadcast_multiply_fusion, f32[256,256]{1,0:T(8,128)S(1)} %copy-done.1, f32[2]{0:T(128)S(1)} %fusion.64), kind=kLoop, calls=%fused_computation.141 | loop fusion | flops 1441792 | bytes 3145736 | tf_op jit(solution)/shard_map/convert
  124.7 11.7 %collective-permute-done = bf16[2,256,512]{2,1,0:T(8,128)(2,1)S(1)} collective-permute-done((bf16[2,256,512]{2,1,0:T(8,128)(2,1)}, bf16[2,256,512]{2,1,0:T(8,128)(2,1)S(1)}, u32[]{:S(2)}, u32[]{:S(2)}) %collective-permute-start) | collective-permute-done | bytes 524320 | tf_op jit(solution)/shard_map/while/body/eval_jaxpr/ppermute | solution.py:12
  137.7 25.3 %conditional.6 = (bf16[2,256,512]{2,1,0:T(8,128)(2,1)}, f32[256,2,256]{2,0,1:T(8,128)S(1)}) conditional(s32[]{:T(128)} %convert_element_type.155, () %tuple.108, (pred[]{:T(512)}, bf16[2,256,512]{2,1,0:T(8,128)(2,1)S(1)}, bf16[2,256,512]{2,1,0:T(8,128)(2,1)S(1)}, bf16[512,512]{1,0:T(8,128)(2,1)S(1)}, f32[1,3]{1,0:T(1,128)S(1)}, ...), branch_computations={%region_1.1_spmd, %region_2.4_spmd.clone} | conditional | flops 2162033664 | bytes 46668028 | solution.py:160
  143.4 2.7 %subtract_convert_fusion.1 = (bf16[2,256,256]{2,1,0:T(8,128)(2,1)S(1)}, bf16[2,256,256]{2,1,0:T(8,128)(2,1)S(1)}) fusion(f32[2,256,512]{2,1,0:T(8,128)S(1)} %fusion.55, f32[2]{0:T(128)S(1)} %copy-done.3, f32[256,256]{1,0:T(8,128)S(1)} %broadcast_add_fusion, f32[2]{0:T(128)S(1)} %get-tuple-element.564), kind=kLoop, calls=%fused_computation.74 | loop fusion | flops 2097152 | bytes 1835024 | tf_op jit(solution)/shard_map/convert.13
  150.0 2.1 %fusion.86 = (bf16[2,256,256]{2,1,0:T(8,128)(2,1)S(1)}, f32[2,256,256]{2,1,0:T(8,128)S(1)}, bf16[2,256,256]{2,1,0:T(8,128)(2,1)S(1)}, f32[2,256,256]{2,1,0:T(8,128)S(1)}) fusion(f32[2,256,512]{2,1,0:T(8,128)S(1)} %convolution_multiply_fusion.2, f32[256,256]{1,0:T(8,128)S(1)} %broadcast_multiply_fusion, f32[256,256]{1,0:T(8,128)S(1)} %get-tuple-element.560, ...), kind=kLoop, calls=%fused_computation.143 | loop fusion | flops 1441792 | bytes 3145736 | tf_op jit(solution)/shard_map/convert.9
  154.6 2.7 %subtract_convert_fusion = (bf16[2,256,256]{2,1,0:T(8,128)(2,1)S(1)}, bf16[2,256,256]{2,1,0:T(8,128)(2,1)S(1)}) fusion(f32[2,256,512]{2,1,0:T(8,128)S(1)} %fusion.53, f32[2]{0:T(128)S(1)} %get-tuple-element.563, f32[2]{0:T(128)S(1)} %copy-done.3, f32[256,256]{1,0:T(8,128)S(1)} %broadcast_add_fusion), kind=kLoop, calls=%fused_computation.72 | loop fusion | flops 2097152 | bytes 1835024 | tf_op jit(solution)/shard_map/convert.5
  159.9 2.1 %fusion.82 = (bf16[2,256,256]{2,1,0:T(8,128)(2,1)S(1)}, f32[2,256,256]{2,1,0:T(8,128)S(1)}, bf16[2,256,256]{2,1,0:T(8,128)(2,1)S(1)}, f32[2,256,256]{2,1,0:T(8,128)S(1)}) fusion(f32[2,256,512]{2,1,0:T(8,128)S(1)} %convolution_multiply_fusion, f32[256,256]{1,0:T(8,128)S(1)} %broadcast_multiply_fusion, f32[256,256]{1,0:T(8,128)S(1)} %copy-done.1, f32[2]{0:T(128)S(1)} %fusion.64), kind=kLoop, calls=%fused_computation.141 | loop fusion | flops 1441792 | bytes 3145736 | tf_op jit(solution)/shard_map/convert
  166.2 10.8 %collective-permute-done = bf16[2,256,512]{2,1,0:T(8,128)(2,1)S(1)} collective-permute-done((bf16[2,256,512]{2,1,0:T(8,128)(2,1)}, bf16[2,256,512]{2,1,0:T(8,128)(2,1)S(1)}, u32[]{:S(2)}, u32[]{:S(2)}) %collective-permute-start) | collective-permute-done | bytes 524320 | tf_op jit(solution)/shard_map/while/body/eval_jaxpr/ppermute | solution.py:12
  179.6 7.5 %reduce-scatter.4.cloned.1.call-done = bf16[128,512]{1,0:T(8,128)(2,1)} async-done(((bf16[256,512]{1,0:T(8,128)(2,1)}), bf16[128,512]{1,0:T(8,128)(2,1)}) %reduce-scatter.4.cloned.1.call-update) | async-done | bytes 131088
  189.1 13.8 %all_to_all.5 = bf16[4,128,2,128]{3,1,2,0:T(8,128)(2,1)S(1)} all-to-all(bf16[4,128,2,128]{3,1,2,0:T(8,128)(2,1)S(1)} %copy.33), channel_id=1, replica_groups=mesh['groups'=2,'shot'=4,'depth'=2,'freq'=2] {'shot'}, dimensions={0} | all-to-all | bytes 524288 | tf_op jit(solution)/shard_map/all_to_all | solution.py:184
  (165 shorter events, 67.3 us)
Async XLA Ops:
  6.5 4.5 %copy-start.2 = (f32[1,3,2,256,256]{4,3,2,1,0:T(8,128)S(1)}, f32[1,3,2,256,256]{4,3,2,1,0:T(8,128)}, u32[]{:S(2)}) copy-start(f32[1,3,2,256,256]{4,3,2,1,0:T(8,128)} %param.11) | copy-start | bytes 4718596
  6.5 180.6 %reduce-scatter.4.cloned.1.call-start = ((), (), s32[]{:S(2)}) async-start(), calls=%async_computation.2 | async-start | bytes 393216
  12.0 1.0 copy-start
  12.0 1.0 copy-start.4
  15.2 37.5 %collective-permute-start = (bf16[2,256,512]{2,1,0:T(8,128)(2,1)}, bf16[2,256,512]{2,1,0:T(8,128)(2,1)S(1)}, u32[]{:S(2)}, u32[]{:S(2)}) collective-permute-start(bf16[2,256,512]{2,1,0:T(8,128)(2,1)} %get-tuple-element.656), channel_id=1, source_target_pairs={{0,2},{1,3},{4,6},{5,7},{8,10},{9,11},{12,14},{13,15},{16,18},{17,... | collective-permute-start | bytes 1572872 | tf_op jit(solution)/shard_map/while/body/eval_jaxpr/ppermute | solution.py:12
  58.8 0.9 copy-start.3
  75.1 1.0 copy-start.1
  79.2 15.8 %collective-permute-start = (bf16[2,256,512]{2,1,0:T(8,128)(2,1)}, bf16[2,256,512]{2,1,0:T(8,128)(2,1)S(1)}, u32[]{:S(2)}, u32[]{:S(2)}) collective-permute-start(bf16[2,256,512]{2,1,0:T(8,128)(2,1)} %get-tuple-element.656), channel_id=1, source_target_pairs={{0,2},{1,3},{4,6},{5,7},{8,10},{9,11},{12,14},{13,15},{16,18},{17,... | collective-permute-start | bytes 1572872 | tf_op jit(solution)/shard_map/while/body/eval_jaxpr/ppermute | solution.py:12
  101.1 0.9 copy-start.3
  117.5 1.0 copy-start.1
  121.5 14.9 %collective-permute-start = (bf16[2,256,512]{2,1,0:T(8,128)(2,1)}, bf16[2,256,512]{2,1,0:T(8,128)(2,1)S(1)}, u32[]{:S(2)}, u32[]{:S(2)}) collective-permute-start(bf16[2,256,512]{2,1,0:T(8,128)(2,1)} %get-tuple-element.656), channel_id=1, source_target_pairs={{0,2},{1,3},{4,6},{5,7},{8,10},{9,11},{12,14},{13,15},{16,18},{17,... | collective-permute-start | bytes 1572872 | tf_op jit(solution)/shard_map/while/body/eval_jaxpr/ppermute | solution.py:12
  142.5 0.9 copy-start.3
  158.9 1.0 copy-start.1
  163.0 14.0 %collective-permute-start = (bf16[2,256,512]{2,1,0:T(8,128)(2,1)}, bf16[2,256,512]{2,1,0:T(8,128)(2,1)S(1)}, u32[]{:S(2)}, u32[]{:S(2)}) collective-permute-start(bf16[2,256,512]{2,1,0:T(8,128)(2,1)} %get-tuple-element.656), channel_id=1, source_target_pairs={{0,2},{1,3},{4,6},{5,7},{8,10},{9,11},{12,14},{13,15},{16,18},{17,... | collective-permute-start | bytes 1572872 | tf_op jit(solution)/shard_map/while/body/eval_jaxpr/ppermute | solution.py:12
Sparse Core Ops, SparseCore 0:
  179.1 8.0 reduce-scatter.3
where the time goes:
time: 213 us; the launch traced here: 211 us
  waiting for transfers between devices  77.9 us (37%)
  other arithmetic  55.5 us (26%)
  local copies, waits for them, and re-layouts  28.8 us (14%)
  between operations  14.1 us (7%)
  blocking collectives  13.8 us (6%)
  matrix products  10.4 us (5%)
  starting transfers between devices  5.13 us (2%)
  loops' own time  4.77 us (2%)
    ppermute x4, waiting for transfers between devices, from_behind(): return lax.ppermute(array, axis, pairs)  70.4 us
    another operation x16, other arithmetic  29.4 us
    all_to_all x1, blocking collectives, local(): lax.all_to_all(blocks.astype(jnp.bfloat16), 'shot', split_axis=0, concat_...  13.8 us
    transpose x12, local copies, waits for them, and re-layouts, flip_parts(): moved = jnp.swapaxes(pieces, -3, -1)  12 us
    unnamed x2, waiting for transfers between devices  7.57 us
    add x4, other arithmetic, one_turn(): return (incoming, image_sum + level_image)  6.64 us
    ppermute x4, starting transfers between devices, from_behind(): return lax.ppermute(array, axis, pairs)  5.13 us
    another operation x4, loops' own time, one_turn(): lax.cond(active, extrapolate_front, stay_still, (begin_field, rate_now))  4.55 us
  transfers between devices with their start and end apart: 5, of which 5 were waited for; matrix products, arithmetic and copies ran while one was open for 3% of the time, Pallas kernels for 0%

commit v1 on v0

--- a/solution.py
+++ b/solution.py
@@ -1,6 +1,12 @@
+import functools
+
 import jax
 import jax.numpy as jnp
+import ml_dtypes
+import numpy as np
 from jax import lax
+from jax.experimental import pallas as pl
+from jax.experimental.pallas import tpu as pltpu
 from jax.sharding import PartitionSpec as P
 
 TILE = 128
@@ -188,9 +194,446 @@
     return collected
 
 
+MESH = pl.DeviceIdType.MESH
+BF16 = jnp.bfloat16
+F32 = jnp.float32
+SLOWEST, SLOWNESS_SPAN, FASTEST_TURN = 1.4, 0.8, 2.5
+
+
+def even_polynomial(function, limit, degree):
+    series = np.polynomial.chebyshev.Chebyshev.interpolate(
+        lambda x: function(np.sqrt(np.maximum(x, 0.0))), degree, domain=[0.0, limit]
+    )
+    return [float(c) for c in series.convert(kind=np.polynomial.Polynomial).coef]
+
+
+def horner(coefficients, x):
+    total = coefficients[-1] * x + coefficients[-2]
+    for c in coefficients[-3::-1]:
+        total = total * x + c
+    return total
+
+
+def sinc(y):
+    return np.sinc(y / np.pi)
+
+
+def fold_order(points):
+    half = points // 2
+    even = list(range(0, half, 2)) + [half] + list(range(points - 2, half, -2))
+    odd = list(range(1, half, 2)) + list(range(points - 1, half, -2))
+    return np.array(even), np.array(odd)
+
+
+def fold_tables(points):
+    half = points // 2
+    positions = np.arange(points)
+    angles = 2.0 * np.pi / points * (positions[:, None] * positions[None, :] % points)
+    cosine, sine = np.cos(angles), np.sin(angles)
+    right_forward, left_forward, left_inverse, right_inverse = [], [], [], []
+    for order in fold_order(points):
+        c, s = cosine[:half, order], sine[:half, order]
+        right_forward.append(np.block([[c, -s], [s, c]]))
+        left_forward.append(np.block([[c.T, s.T], [-s.T, c.T]]))
+        left_inverse.append(np.block([[c, -s], [s, c]]))
+        right_inverse.append(np.block([[c.T, s.T], [-s.T, c.T]]))
+    return [
+        np.stack(t).astype(ml_dtypes.bfloat16)
+        for t in (right_forward, left_forward, left_inverse, right_inverse)
+    ]
+
+
+def fold_grids(points):
+    wrapped = (np.arange(points) + points // 2) % points - points // 2
+    squared = np.square(2.0 * np.pi / points * wrapped)[np.concatenate(fold_order(points))]
+    square = (squared[:, None] + squared[None, :]).astype(np.float32)
+    distance_in = np.minimum(np.arange(points), points - 1 - np.arange(points)) + 1
+    taper = np.minimum(distance_in / (points // 16), 1.0)
+    window = (taper[:, None] * taper[None, :] / points).astype(np.float32)
+    return square, window
+
+
+def migrate_kernel(
+    dims, source, receiver, slowness, omegas, start, rf, lf, li, ri, square, window, image,
+    fbuf, st, stx, ds, s0, om, pr, pi, cr, ci, bb, ww, xx, uq, acc, accb, shq, accr, shr, chip,
+    xsend, xrecv, zsend, zrecv,
+    load_sem, ds_sem, s0_sem, sh_sem, om_sem, acc_sem, shq_sem, x_sem, zs_sem, zr_sem,
+):
+    points, levels, shots, fronts = dims
+    half, quarter = points // 2, points // 4
+    total_levels = 2 * levels
+    d, f, s = lax.axis_index("depth"), lax.axis_index("freq"), lax.axis_index("shot")
+    other_core, other_chip = {"freq": 1 - f}, {"depth": 1 - d}
+    provider = f == d
+
+    barrier = pltpu.get_barrier_semaphore()
+    pl.semaphore_signal(barrier, inc=1, device_id=other_core, device_id_type=MESH)
+    pl.semaphore_signal(barrier, inc=1, device_id=other_chip, device_id_type=MESH)
+    for step in range(1, shots):
+        pl.semaphore_signal(
+            barrier, inc=1, device_id={"shot": lax.rem(s + step, shots)}, device_id_type=MESH
+        )
+
+    def load(index, front, field):
+        return pltpu.make_async_copy(field.at[0, front], fbuf.at[index], load_sem.at[index])
+
+    def remote(source_ref, target_ref, sems, device, index):
+        return pltpu.make_async_remote_copy(
+            src_ref=source_ref, dst_ref=target_ref, send_sem=sems.at[0, index],
+            recv_sem=sems.at[1, index], device_id=device, device_id_type=MESH,
+        )
+
+    def send_field():
+        return remote(stx, st.at[2], sh_sem, other_core, 0)
+
+    def send_turn():
+        return remote(om, om, om_sem, other_core, 0)
+
+    def send_slow(z):
+        return remote(ds.at[z], ds.at[z], ds_sem, other_chip, z)
+
+    def send_mean(z):
+        return remote(s0.at[z], s0.at[z], s0_sem, other_chip, z)
+
+    def send_image(z):
+        return remote(accb.at[z, 1 - f], accr.at[z], acc_sem, other_core, z)
+
+    def send_shared(z):
+        return remote(shq.at[z, 1 - f], shr.at[z], shq_sem, other_core, z)
+
+    def send_section(z):
+        j = lax.rem(z, levels)
+        return remote(xsend.at[j], xrecv.at[j], x_sem, other_chip, j)
+
+    def send_columns(j, step):
+        owner = lax.rem(s + step, shots)
+        return pltpu.make_async_remote_copy(
+            src_ref=zsend.at[j, owner], dst_ref=zrecv.at[j, s], send_sem=zs_sem.at[j, owner],
+            recv_sem=zr_sem.at[j, s], device_id={"shot": owner}, device_id_type=MESH,
+        )
+
+    def recv_columns(j, step):
+        owner = lax.rem(s + step, shots)
+        return pltpu.make_async_remote_copy(
+            src_ref=zsend.at[j, owner], dst_ref=zrecv.at[j, owner], send_sem=zs_sem.at[j, owner],
+            recv_sem=zr_sem.at[j, owner], device_id={"shot": owner}, device_id_type=MESH,
+        )
+
+    load(0, d, source).start()
+    load(1, d, receiver).start()
+
+    @pl.when(provider)
+    def _():
+        load(2, fronts - 1, source).start()
+        load(3, fronts - 1, receiver).start()
+
+    for j in range(levels):
+        mean = jnp.mean(slowness[0, j])
+        ds[d * levels + j] = (slowness[0, j] - mean).astype(BF16)
+        s0[d * levels + j] = jnp.full((8, points), mean, F32)
+
+    pl.semaphore_wait(barrier, shots + 1)
+    for j in range(levels):
+        send_mean(d * levels + j).start()
+        send_slow(d * levels + j).start()
+
+    def fold_into(target, re, im):
+        lo, hi = slice(0, half), slice(half, points)
+        target[0, :, lo] = (re[:, lo] + re[:, hi]).astype(BF16)
+        target[0, :, hi] = (im[:, lo] + im[:, hi]).astype(BF16)
+        target[1, :, lo] = (re[:, lo] - re[:, hi]).astype(BF16)
+        target[1, :, hi] = (im[:, lo] - im[:, hi]).astype(BF16)
+
+    @pl.when(provider)
+    def _():
+        om[...] = jnp.full((8, points), omegas[0, fronts - 1], F32)
+        send_turn().start()
+        load(2, fronts - 1, source).wait()
+        load(3, fronts - 1, receiver).wait()
+        fold_into(stx, fbuf[3 - f, 0], fbuf[3 - f, 1])
+        send_field().start()
+        fold_into(st.at[2], fbuf[2 + f, 0], fbuf[2 + f, 1])
+
+    for index, field in enumerate((source, receiver)):
+        load(index, d, field).wait()
+        fold_into(st.at[index], fbuf[index, 0], fbuf[index, 1])
+
+    @pl.when(jnp.logical_not(provider))
+    def _():
+        send_turn().wait_recv()
+        send_field().wait_recv()
+
+    turn_own = omegas[0, d]
+    sign = (2 * f - 1).astype(F32)
+    limit = 1.01 * (FASTEST_TURN * SLOWEST) ** 2
+    kz_cos = even_polynomial(np.cos, limit, 6)
+    kz_sinc = even_polynomial(sinc, limit, 6)
+    limit = 1.01 * (FASTEST_TURN * SLOWNESS_SPAN) ** 2
+    turn_cos = even_polynomial(np.cos, limit, 4)
+    turn_sinc = even_polynomial(sinc, limit, 4)
+    inv = 1.0 / points
+
+    def propagator(index, radius_sq, flip):
+        def rows(at, count, targets):
+            vertical = radius_sq - square[at : at + count, :]
+            root = jnp.sqrt(jnp.abs(vertical))
+            positive = vertical >= 0.0
+            x = jnp.maximum(vertical, 0.0)
+            re = jnp.where(positive, horner(kz_cos, x), jnp.exp(-root)) * inv
+            im = jnp.where(positive, root * horner(kz_sinc, x), 0.0) * (inv * flip)
+            for target in targets:
+                pr[index, target : target + count, :] = re
+                pi[index, target : target + count, :] = im
+
+        step = quarter // 2
+        for at in range(0, quarter, step):
+            rows(at, step, (at, at + quarter))
+            rows(half + at, step, (half + at, half + quarter + at))
+        rows(quarter, 8, (quarter,))
+
+    def correction(index, turn, slow):
+        step = quarter // 2
+        for at in range(0, points, step):
+            x = turn * slow[at : at + step, :].astype(F32)
+            y = x * x
+            w = window[at : at + step, :]
+            cr[index, at : at + step, :] = horner(turn_cos, y) * w
+            ci[index, at : at + step, :] = horner(turn_sinc, y) * (x * w)
+
+    def dot(a, b):
+        return jnp.dot(a, b, preferred_element_type=F32)
+
+    def transform(i):
+        for part in range(2):
+            v = dot(st[i, part], rf[part])
+            top, bottom = v[:half], v[half:]
+            lanes = slice(part * half, (part + 1) * half)
+            for fold, w in ((0, top + bottom), (1, top - bottom)):
+                bb[i, fold, :half, lanes] = w[:, :half].astype(BF16)
+                bb[i, fold, half:, lanes] = w[:, half:].astype(BF16)
+
+    def advance(i, which, sigma):
+        for part in range(2):
+            w = dot(lf[part], bb[i, part])
+            rows = slice(part * half, (part + 1) * half)
+            re, im = w[:half], w[half:]
+            p, q = pr[which, rows, :], pi[which, rows, :]
+            if sigma > 0:
+                ww[i, part, :half, :] = (re * p - im * q).astype(BF16)
+                ww[i, part, half:, :] = (re * q + im * p).astype(BF16)
+            else:
+                ww[i, part, :half, :] = (re * p + im * q).astype(BF16)
+                ww[i, part, half:, :] = (im * p - re * q).astype(BF16)
+
+    def back(i):
+        even, odd = dot(li[0], ww[i, 0]), dot(li[1], ww[i, 1])
+        for rows, y in ((slice(0, half), even + odd), (slice(half, points), even - odd)):
+            for part in range(2):
+                lanes = slice(part * half, (part + 1) * half)
+                xx[i, part, rows, :half] = y[:half, lanes].astype(BF16)
+                xx[i, part, rows, half:] = y[half:, lanes].astype(BF16)
+
+    def finish(i, which, sigma):
+        even, odd = dot(xx[i, 0], ri[0]), dot(xx[i, 1], ri[1])
+        out = []
+        for lanes, y in ((slice(0, half), even + odd), (slice(half, points), even - odd)):
+            re, im = y[:, :half], y[:, half:]
+            c, t = cr[which, :, lanes], ci[which, :, lanes]
+            if sigma > 0:
+                out.append((re * c - im * t, re * t + im * c))
+            else:
+                out.append((re * c + im * t, im * c - re * t))
+        for fold in range(2):
+            for which_part in range(2):
+                a, b = out[0][which_part], out[1][which_part]
+                lanes = slice(which_part * half, (which_part + 1) * half)
+                st[i, fold, :, lanes] = (a + b if fold == 0 else a - b).astype(BF16)
+        return out
+
+    def combine(z):
+        send_image(z).wait_recv()
+        send_shared(z).wait_recv()
+        total = acc[lax.rem(z, 2), f] + accr[z].astype(F32)
+        total += shq[z, f, 0].astype(F32) * shr[z, 0].astype(F32)
+        total += shq[z, f, 1].astype(F32) * shr[z, 1].astype(F32)
+        mine = lax.div(z, levels) == d
+
+        @pl.when(mine)
+        def _():
+            chip[lax.rem(z, levels)] = total
+
+        @pl.when(jnp.logical_not(mine))
+        def _():
+            xsend[lax.rem(z, levels)] = total.astype(BF16)
+            send_section(z).start()
+
+    def place(z):
+        j = lax.rem(z, levels)
+        send_section(z).wait_recv()
+        total = (chip[j] + xrecv[j].astype(F32)).astype(BF16)
+        columns = lax.broadcasted_iota(jnp.int32, (TILE, points), 0)
+        places = lax.broadcasted_iota(jnp.int32, (TILE, points), 1)
+        for owner in range(shots):
+            chosen = places == columns + (owner * TILE - start[0])
+            chosen = jnp.where(chosen, 1.0, 0.0).astype(BF16)
+            zsend[j, owner] = dot(chosen, total).astype(BF16)
+        for step in range(1, shots):
+            send_columns(j, step).start()
+
+    def one_level(z, carry):
+        mine = lax.div(z, levels) == d
+
+        @pl.when(jnp.logical_not(mine))
+        def _():
+            send_mean(z).wait_recv()
+            send_slow(z).wait_recv()
+
+        mean = s0[z][0:1, :]
+        turn_shared = om[0:1, :]
+        transform(2)
+        propagator(1, jnp.square(turn_shared * mean), sign)
+        correction(1, sign * turn_shared, ds[z])
+        transform(0)
+        transform(1)
+        propagator(0, jnp.square(turn_own * mean), 1.0)
+        correction(0, turn_own, ds[z])
+        advance(2, 1, 1)
+        back(2)
+        advance(0, 0, -1)
+        advance(1, 0, 1)
+
+        @pl.when(z >= 1)
+        def _():
+            combine(z - 1)
+
+        shared = finish(2, 1, 1)
+        for side in range(2):
+            for part in range(2):
+                shq[z, side, part] = shared[side][part].astype(BF16)
+        send_shared(z).start()
+        back(0)
+        back(1)
+        first = finish(0, 0, -1)
+        for side in range(2):
+            for part in range(2):
+                uq[side, part] = first[side][part]
+        second = finish(1, 0, 1)
+        for side in range(2):
+            product = uq[side, 0] * second[side][0] + uq[side, 1] * second[side][1]
+            acc[lax.rem(z, 2), side] = product
+            accb[z, side] = product.astype(BF16)
+        send_image(z).start()
+
+        @pl.when(jnp.logical_and(z >= 1, lax.div(z - 1, levels) == d))
+        def _():
+            place(z - 1)
+
+        return carry
+
+    lax.fori_loop(0, total_levels, one_level, 0)
+    last = total_levels - 1
+    combine(last)
+
+    @pl.when(lax.div(last, levels) == d)
+    def _():
+        place(last)
+
+    for j in range(levels):
+        total = zsend[j, s].astype(F32)
+        for step in range(1, shots):
+            recv_columns(j, step).wait_recv()
+            total += zrecv[j, lax.rem(s + step, shots)].astype(F32)
+        image[:, j, :] = total
+
+    @pl.when(provider)
+    def _():
+        send_turn().wait_send()
+        send_field().wait_send()
+
+    for j in range(levels):
+        send_mean(d * levels + j).wait_send()
+        send_slow(d * levels + j).wait_send()
+        send_section((1 - d) * levels + j).wait_send()
+        for step in range(1, shots):
+            send_columns(j, step).wait_send()
+    for z in range(total_levels):
+        send_image(z).wait_send()
+        send_shared(z).wait_send()
+
+
+def migrate(source, receiver, slowness, omegas, shot_start):
+    points = source.shape[-1]
+    fronts = source.shape[1]
+    levels = slowness.shape[1]
+    shots = lax.axis_size("shot")
+    total = 2 * levels
+    half = points // 2
+    tables_in = [jnp.asarray(t) for t in fold_tables(points)]
+    grids_in = [jnp.asarray(t) for t in fold_grids(points)]
+    full = (points, points)
+    side = (points, half)
+    vmem, sem = pltpu.VMEM, pltpu.SemaphoreType.DMA
+    in_vmem = pl.BlockSpec(memory_space=pltpu.VMEM)
+    in_smem = pl.BlockSpec(memory_space=pltpu.SMEM)
+    anywhere = pl.BlockSpec(memory_space=pl.ANY)
+    return pl.pallas_call(
+        functools.partial(migrate_kernel, (points, levels, shots, fronts)),
+        out_shape=jax.ShapeDtypeStruct((TILE, levels, half), F32),
+        in_specs=[anywhere, anywhere, in_vmem, in_smem, in_smem] + [in_vmem] * 6,
+        out_specs=in_vmem,
+        scratch_shapes=[
+            vmem((4, 2) + full, F32),
+            vmem((3, 2) + full, BF16),
+            vmem((2,) + full, BF16),
+            vmem((total,) + full, BF16),
+            vmem((total, 8, points), F32),
+            vmem((8, points), F32),
+            vmem((2,) + full, F32),
+            vmem((2,) + full, F32),
+            vmem((2,) + full, F32),
+            vmem((2,) + full, F32),
+            vmem((3, 2) + full, BF16),
+            vmem((3, 2) + full, BF16),
+            vmem((3, 2) + full, BF16),
+            vmem((2, 2) + side, F32),
+            vmem((2, 2) + side, F32),
+            vmem((total, 2) + side, BF16),
+            vmem((total, 2, 2) + side, BF16),
+            vmem((total,) + side, BF16),
+            vmem((total, 2) + side, BF16),
+            vmem((levels,) + side, F32),
+            vmem((levels,) + side, BF16),
+            vmem((levels,) + side, BF16),
+            vmem((levels, shots, TILE, half), BF16),
+            vmem((levels, shots, TILE, half), BF16),
+            sem((4,)),
+            sem((2, total)),
+            sem((2, total)),
+            sem((2, 1)),
+            sem((2, 1)),
+            sem((2, total)),
+            sem((2, total)),
+            sem((2, levels)),
+            sem((levels, shots)),
+            sem((levels, shots)),
+        ],
+        compiler_params=pltpu.CompilerParams(
+            collective_id=0, has_side_effects=True, vmem_limit_bytes=48 * 1024 * 1024
+        ),
+        name="migrate",
+    )(source, receiver, slowness, omegas, shot_start, *tables_in, *grids_in)
+
+
 def solution(mesh):
+    sizes = mesh.shape
+
+    def per_device(source, *rest):
+        if sizes["depth"] == 2 and sizes["freq"] == 2 and source.shape[1] == 3:
+            return migrate(source, *rest)
+        return local(source, *rest)
+
     return jax.shard_map(
-        local,
+        per_device,
         mesh=mesh,
         in_specs=(
             P(("groups", "shot"), "freq", None, None, None),

time: 213 us -> 41.2 us (0.19)
  waiting for transfers between devices: 77.9 us -> 0 us
  other arithmetic: 55.5 us -> 0 us
  Pallas kernels: 0 us -> 31.2 us
  local copies, waits for them, and re-layouts: 28.8 us -> 8.96 us
  blocking collectives: 13.8 us -> 0 us
  between operations: 14.1 us -> 0.68 us
  matrix products: 10.4 us -> 0 us
  starting transfers between devices: 5.13 us -> 0 us
  loops' own time: 4.77 us -> 0 us
    ppermute x4 -> x0, waiting for transfers between devices: 70.4 us -> none  [from_behind(): return lax.ppermute(array, axis, pairs)]
    pallas_call x0 -> x1, Pallas kernels: none -> 31.2 us  [migrate(): pl.pallas_call(functools.partial(migrate_kernel, (points, levels, shots,...]
    another operation x19 -> x0, other arithmetic: 29.5 us -> none
    all_to_all x1 -> x0, blocking collectives: 13.8 us -> none  [local(): lax.all_to_all(blocks.astype(jnp.bfloat16), 'shot', split_axis=0, concat_...]
    transpose x12 -> x0, local copies, waits for them, and re-layouts: 12 us -> none  [flip_parts(): moved = jnp.swapaxes(pieces, -3, -1)]
    dot_general x24 -> x0, matrix products: 10.4 us -> none  [the longest x6 2.62 us: extrapolate(): jnp.dot(shifted.reshape(batch_size * points, width), inverse, preferred_e...]
    unnamed x2 -> x0, waiting for transfers between devices: 7.57 us -> none
    add x13 -> x0, other arithmetic: 7.34 us -> none  [the longest x4 6.64 us: one_turn(): return (incoming, image_sum + level_image)]
  transfers between devices with their start and end apart: 5 -> 0, of which waited for: 5 -> 0; matrix products, arithmetic and copies ran while one was open for 3% -> 0% of each run, Pallas kernels for 0% -> 0%
where the time goes in v1:
time: 41.2 us; the launch traced here: 40.8 us
  Pallas kernels  31.2 us (76%)
  local copies, waits for them, and re-layouts  8.96 us (22%)
  between operations  0.68 us (2%)
    pallas_call x1, Pallas kernels, migrate(): pl.pallas_call(functools.partial(migrate_kernel, (points, levels, shots,...  31.2 us
    unnamed x17, local copies, waits for them, and re-layouts  8.96 us

profile of v1, /device:TPU:2, one launch (start us, length us, event | category | flops | bytes accessed | tf_op | source)
XLA Modules:
  0.0 40.8 jit_solution(10955215848081103644)
XLA Ops:
  0.7 0.0 copy-start
  0.7 1.4 %copy-done = f32[1,3,2,256,256]{4,3,2,1,0:T(8,128)S(1)} copy-done((f32[1,3,2,256,256]{4,3,2,1,0:T(8,128)S(1)}, f32[1,3,2,256,256]{4,3,2,1,0:T(8,128)}, u32[]{:S(2)}) %copy-start) | copy-done | bytes 1572888
  2.1 0.0 copy-start.1
  2.1 1.4 %copy-done.1 = f32[1,3,2,256,256]{4,3,2,1,0:T(8,128)S(1)} copy-done((f32[1,3,2,256,256]{4,3,2,1,0:T(8,128)S(1)}, f32[1,3,2,256,256]{4,3,2,1,0:T(8,128)}, u32[]{:S(2)}) %copy-start.1) | copy-done | bytes 1572888
  3.5 0.0 copy-start.2
  3.5 0.9 %copy-done.2 = bf16[2,256,256]{2,1,0:T(8,128)(2,1)S(1)} copy-done((bf16[2,256,256]{2,1,0:T(8,128)(2,1)S(1)}, bf16[2,256,256]{2,1,0:T(8,128)(2,1)}, u32[]{:S(2)}) %copy-start.2) | copy-done | bytes 262168
  4.4 0.0 copy-start.3
  4.4 0.9 %copy-done.3 = bf16[2,256,256]{2,1,0:T(8,128)(2,1)S(1)} copy-done((bf16[2,256,256]{2,1,0:T(8,128)(2,1)S(1)}, bf16[2,256,256]{2,1,0:T(8,128)(2,1)}, u32[]{:S(2)}) %copy-start.3) | copy-done | bytes 262168
  5.4 0.0 copy-start.4
  5.4 1.0 %copy-done.4 = f32[1,2,256,256]{3,2,1,0:T(8,128)S(1)} copy-done((f32[1,2,256,256]{3,2,1,0:T(8,128)S(1)}, f32[1,2,256,256]{3,2,1,0:T(8,128)}, u32[]{:S(2)}) %copy-start.4) | copy-done | bytes 524312
  6.4 0.0 copy-start.5
  6.4 0.9 %copy-done.5 = f32[256,256]{1,0:T(8,128)S(1)} copy-done((f32[256,256]{1,0:T(8,128)S(1)}, f32[256,256]{1,0:T(8,128)}, u32[]{:S(2)}) %copy-start.5) | copy-done | bytes 262168
  7.4 0.0 copy-start.6
  7.4 0.9 %copy-done.6 = f32[256,256]{1,0:T(8,128)S(1)} copy-done((f32[256,256]{1,0:T(8,128)S(1)}, f32[256,256]{1,0:T(8,128)}, u32[]{:S(2)}) %copy-start.6) | copy-done | bytes 262168
  8.3 0.0 copy-start.7
  8.3 0.7 %copy-done.7 = f32[1,3]{1,0:T(1,128)S(1)} copy-done((f32[1,3]{1,0:T(1,128)S(1)}, f32[1,3]{1,0:T(1,128)}, u32[]{:S(2)}) %copy-start.7) | copy-done | bytes 36
  9.0 31.2 %migrate.1 = f32[128,2,128]{2,1,0:T(2,128)S(1)} custom-call(f32[1,3,2,256,256]{4,3,2,1,0:T(8,128)S(1)} %copy-done, f32[1,3,2,256,256]{4,3,2,1,0:T(8,128)S(1)} %copy-done.1, f32[1,2,256,256]{3,2,1,0:T(8,128)S(1)} %copy-done.4, f32[1,3]{1,0:T(1,128)S(1)} %copy-done.7, s32[1]{0:T(128)S(6)} %copy.13.start, bf16[2,256,256]{2,1,0:T(8,128)(2,1)S(1)} %copy-done.3, ...), custom_call_target="tpu_custom_call" | custom-call | tf_op jit(solution)/shard_map/migrate/pallas_call | solution.py:579
  40.2 0.7 %copy.14 = f32[128,2,128]{2,1,0:T(2,128)} copy(f32[128,2,128]{2,1,0:T(2,128)S(1)} %migrate.1) | data formatting | bytes 262144
Async XLA Ops:
  0.7 1.4 %copy-start = (f32[1,3,2,256,256]{4,3,2,1,0:T(8,128)S(1)}, f32[1,3,2,256,256]{4,3,2,1,0:T(8,128)}, u32[]{:S(2)}) copy-start(f32[1,3,2,256,256]{4,3,2,1,0:T(8,128)} %source.1) | copy-start | bytes 4718596
  2.1 1.4 %copy-start.1 = (f32[1,3,2,256,256]{4,3,2,1,0:T(8,128)S(1)}, f32[1,3,2,256,256]{4,3,2,1,0:T(8,128)}, u32[]{:S(2)}) copy-start(f32[1,3,2,256,256]{4,3,2,1,0:T(8,128)} %receiver.1) | copy-start | bytes 4718596
  3.5 0.9 %copy-start.2 = (bf16[2,256,256]{2,1,0:T(8,128)(2,1)S(1)}, bf16[2,256,256]{2,1,0:T(8,128)(2,1)}, u32[]{:S(2)}) copy-start(bf16[2,256,256]{2,1,0:T(8,128)(2,1)} %constant.9.clone.lf.ri) | copy-start | bytes 786436
  4.4 0.9 %copy-start.3 = (bf16[2,256,256]{2,1,0:T(8,128)(2,1)S(1)}, bf16[2,256,256]{2,1,0:T(8,128)(2,1)}, u32[]{:S(2)}) copy-start(bf16[2,256,256]{2,1,0:T(8,128)(2,1)} %constant.8.clone.rf.li) | copy-start | bytes 786436
  5.4 1.0 %copy-start.4 = (f32[1,2,256,256]{3,2,1,0:T(8,128)S(1)}, f32[1,2,256,256]{3,2,1,0:T(8,128)}, u32[]{:S(2)}) copy-start(f32[1,2,256,256]{3,2,1,0:T(8,128)} %slowness.1) | copy-start | bytes 1572868
  6.4 0.9 %copy-start.5 = (f32[256,256]{1,0:T(8,128)S(1)}, f32[256,256]{1,0:T(8,128)}, u32[]{:S(2)}) copy-start(f32[256,256]{1,0:T(8,128)} %constant.11.clone.window) | copy-start | bytes 786436
  7.4 0.9 %copy-start.6 = (f32[256,256]{1,0:T(8,128)S(1)}, f32[256,256]{1,0:T(8,128)}, u32[]{:S(2)}) copy-start(f32[256,256]{1,0:T(8,128)} %constant.10.clone.square) | copy-start | bytes 786436
  8.3 0.7 %copy-start.7 = (f32[1,3]{1,0:T(1,128)S(1)}, f32[1,3]{1,0:T(1,128)}, u32[]{:S(2)}) copy-start(f32[1,3]{1,0:T(1,128)} %omegas.1) | copy-start | bytes 40

commit v2 on v1

--- a/solution.py
+++ b/solution.py
@@ -2,7 +2,6 @@
 
 import jax
 import jax.numpy as jnp
-import ml_dtypes
 import numpy as np
 from jax import lax
 from jax.experimental import pallas as pl
@@ -196,6 +195,7 @@
 
 MESH = pl.DeviceIdType.MESH
 BF16 = jnp.bfloat16
+CHUNK = 32
 F32 = jnp.float32
 SLOWEST, SLOWNESS_SPAN, FASTEST_TURN = 1.4, 0.8, 2.5
 
@@ -218,46 +218,11 @@
     return np.sinc(y / np.pi)
 
 
-def fold_order(points):
-    half = points // 2
-    even = list(range(0, half, 2)) + [half] + list(range(points - 2, half, -2))
-    odd = list(range(1, half, 2)) + list(range(points - 1, half, -2))
-    return np.array(even), np.array(odd)
-
-
-def fold_tables(points):
-    half = points // 2
-    positions = np.arange(points)
-    angles = 2.0 * np.pi / points * (positions[:, None] * positions[None, :] % points)
-    cosine, sine = np.cos(angles), np.sin(angles)
-    right_forward, left_forward, left_inverse, right_inverse = [], [], [], []
-    for order in fold_order(points):
-        c, s = cosine[:half, order], sine[:half, order]
-        right_forward.append(np.block([[c, -s], [s, c]]))
-        left_forward.append(np.block([[c.T, s.T], [-s.T, c.T]]))
-        left_inverse.append(np.block([[c, -s], [s, c]]))
-        right_inverse.append(np.block([[c.T, s.T], [-s.T, c.T]]))
-    return [
-        np.stack(t).astype(ml_dtypes.bfloat16)
-        for t in (right_forward, left_forward, left_inverse, right_inverse)
-    ]
-
-
-def fold_grids(points):
-    wrapped = (np.arange(points) + points // 2) % points - points // 2
-    squared = np.square(2.0 * np.pi / points * wrapped)[np.concatenate(fold_order(points))]
-    square = (squared[:, None] + squared[None, :]).astype(np.float32)
-    distance_in = np.minimum(np.arange(points), points - 1 - np.arange(points)) + 1
-    taper = np.minimum(distance_in / (points // 16), 1.0)
-    window = (taper[:, None] * taper[None, :] / points).astype(np.float32)
-    return square, window
-
-
 def migrate_kernel(
-    dims, source, receiver, slowness, omegas, start, rf, lf, li, ri, square, window, image,
-    fbuf, st, stx, ds, s0, om, pr, pi, cr, ci, bb, ww, xx, uq, acc, accb, shq, accr, shr, chip,
+    dims, source, receiver, slowness, omegas, start, image,
+    tab, slow, square, window, res, fbuf, st, ds, s0, om, pr, pi, cr, ci, bb, ww, xx, uq, acc, accb, shq, accr, shr, chip,
     xsend, xrecv, zsend, zrecv,
-    load_sem, ds_sem, s0_sem, sh_sem, om_sem, acc_sem, shq_sem, x_sem, zs_sem, zr_sem,
+    load_sem, slow_sem, ds_sem, s0_sem, sh_sem, om_sem, acc_sem, shq_sem, x_sem, zs_sem, zr_sem,
 ):
     points, levels, shots, fronts = dims
     half, quarter = points // 2, points // 4
@@ -284,7 +249,13 @@
         )
 
     def send_field():
-        return remote(stx, st.at[2], sh_sem, other_core, 0)
+        return send_front(source)
+
+    def send_front(field):
+        return remote(field.at[0, fronts - 1], fbuf.at[2], sh_sem, other_core, 0)
+
+    def load_slow(j):
+        return pltpu.make_async_copy(slowness.at[0, j], slow.at[j], slow_sem.at[j])
 
     def send_turn():
         return remote(om, om, om_sem, other_core, 0)
@@ -319,58 +290,106 @@
             recv_sem=zr_sem.at[j, owner], device_id={"shot": owner}, device_id_type=MESH,
         )
 
+    for j in range(levels):
+        load_slow(j).start()
+    for front in range(2):
+        @pl.when(jnp.logical_and(provider, f == front))
+        def _(field=(source, receiver)[front]):
+            load(2, fronts - 1, field).start()
+
     load(0, d, source).start()
     load(1, d, receiver).start()
 
+    def grid_index(axis):
+        at = lax.broadcasted_iota(jnp.int32, (points, points), axis)
+        odd = jnp.where(at >= half, 1, 0)
+        wave = 2 * jnp.where(at - half * odd >= quarter, at - half * odd - quarter, at - half * odd)
+        return at, jnp.where(at == quarter, half, wave + odd).astype(F32) * (2.0 * np.pi / points)
+
+    row, row_wave = grid_index(0)
+    column, column_wave = grid_index(1)
+    square[...] = jnp.square(row_wave) + jnp.square(column_wave)
+
+    table_cos = even_polynomial(np.cos, np.pi**2, 8)
+    table_sinc = even_polynomial(sinc, np.pi**2, 8)
+
+    def frequency(axis, part):
+        at = lax.broadcasted_iota(jnp.int32, (half, half), axis)
+        if part == 1:
+            return jnp.where(at < quarter, 2 * at + 1, points - 1 - 2 * (at - quarter))
+        mirrored = jnp.where(at == quarter, half, points - 2 * (at - quarter))
+        return jnp.where(at < quarter, 2 * at, mirrored)
+
+    for part in range(2):
+        for turned in range(2):
+            place = lax.broadcasted_iota(jnp.int32, (half, half), turned)
+            product = place * frequency(1 - turned, part)
+            wrapped = ((product + half) & (points - 1)) - half
+            x = wrapped.astype(F32) * (2.0 * np.pi / points)
+            cosine = horner(table_cos, x * x).astype(BF16)
+            sine = x * horner(table_sinc, x * x)
+            upper, lower = ((-sine).astype(BF16), sine.astype(BF16))
+            if turned:
+                upper, lower = lower, upper
+            tab[turned, part, :half, :half] = cosine
+            tab[turned, part, half:, half:] = cosine
+            tab[turned, part, :half, half:] = upper
+            tab[turned, part, half:, :half] = lower
+
+    def taper(at):
+        distance_in = (jnp.minimum(at, points - 1 - at) + 1).astype(F32)
+        return jnp.minimum(distance_in * (16.0 / points), 1.0)
+
+    window[...] = taper(row) * taper(column) * (1.0 / points)
+
+    pl.semaphore_wait(barrier, shots + 1)
+    for front in range(2):
+        @pl.when(jnp.logical_and(provider, f == front))
+        def _(field=(receiver, source)[front]):
+            om[...] = jnp.full((8, points), omegas[0, fronts - 1], F32)
+            send_turn().start()
+            send_front(field).start()
+
+    for j in range(levels):
+        load_slow(j).wait()
+        mean = jnp.mean(slow[j])
+        ds[d * levels + j] = (slow[j] - mean).astype(BF16)
+        s0[d * levels + j] = jnp.full((8, points), mean, F32)
+        send_mean(d * levels + j).start()
+        send_slow(d * levels + j).start()
+
+    def fold_into(target, re, im):
+        lo, hi = slice(0, half), slice(half, points)
+        for at in range(0, points, CHUNK):
+            rows = slice(at, at + CHUNK)
+            for lanes, x in ((lo, re), (hi, im)):
+                a, b = x[rows, lo], x[rows, hi]
+                target[0, rows, lanes] = (a + b).astype(BF16)
+                target[1, rows, lanes] = (a - b).astype(BF16)
+
+    for index, field in enumerate((source, receiver)):
+        load(index, d, field).wait()
+        fold_into(st.at[index], fbuf.at[index, 0], fbuf.at[index, 1])
+
     @pl.when(provider)
     def _():
-        load(2, fronts - 1, source).start()
-        load(3, fronts - 1, receiver).start()
-
-    for j in range(levels):
-        mean = jnp.mean(slowness[0, j])
-        ds[d * levels + j] = (slowness[0, j] - mean).astype(BF16)
-        s0[d * levels + j] = jnp.full((8, points), mean, F32)
-
-    pl.semaphore_wait(barrier, shots + 1)
-    for j in range(levels):
-        send_mean(d * levels + j).start()
-        send_slow(d * levels + j).start()
-
-    def fold_into(target, re, im):
-        lo, hi = slice(0, half), slice(half, points)
-        target[0, :, lo] = (re[:, lo] + re[:, hi]).astype(BF16)
-        target[0, :, hi] = (im[:, lo] + im[:, hi]).astype(BF16)
-        target[1, :, lo] = (re[:, lo] - re[:, hi]).astype(BF16)
-        target[1, :, hi] = (im[:, lo] - im[:, hi]).astype(BF16)
-
-    @pl.when(provider)
-    def _():
-        om[...] = jnp.full((8, points), omegas[0, fronts - 1], F32)
-        send_turn().start()
         load(2, fronts - 1, source).wait()
-        load(3, fronts - 1, receiver).wait()
-        fold_into(stx, fbuf[3 - f, 0], fbuf[3 - f, 1])
-        send_field().start()
-        fold_into(st.at[2], fbuf[2 + f, 0], fbuf[2 + f, 1])
-
-    for index, field in enumerate((source, receiver)):
-        load(index, d, field).wait()
-        fold_into(st.at[index], fbuf[index, 0], fbuf[index, 1])
 
     @pl.when(jnp.logical_not(provider))
     def _():
         send_turn().wait_recv()
         send_field().wait_recv()
 
+    fold_into(st.at[2], fbuf.at[2, 0], fbuf.at[2, 1])
+
     turn_own = omegas[0, d]
     sign = (2 * f - 1).astype(F32)
     limit = 1.01 * (FASTEST_TURN * SLOWEST) ** 2
-    kz_cos = even_polynomial(np.cos, limit, 6)
-    kz_sinc = even_polynomial(sinc, limit, 6)
+    kz_cos = even_polynomial(np.cos, limit, 5)
+    kz_sinc = even_polynomial(sinc, limit, 5)
     limit = 1.01 * (FASTEST_TURN * SLOWNESS_SPAN) ** 2
     turn_cos = even_polynomial(np.cos, limit, 4)
-    turn_sinc = even_polynomial(sinc, limit, 4)
+    turn_sinc = even_polynomial(sinc, limit, 3)
     inv = 1.0 / points
 
     def propagator(index, radius_sq, flip):
@@ -405,50 +424,63 @@
 
     def transform(i):
         for part in range(2):
-            v = dot(st[i, part], rf[part])
-            top, bottom = v[:half], v[half:]
+            res[i, part] = dot(st[i, part], tab[0, part])
             lanes = slice(part * half, (part + 1) * half)
-            for fold, w in ((0, top + bottom), (1, top - bottom)):
-                bb[i, fold, :half, lanes] = w[:, :half].astype(BF16)
-                bb[i, fold, half:, lanes] = w[:, half:].astype(BF16)
+            for at in range(0, half, CHUNK):
+                top = res[i, part, at : at + CHUNK, :]
+                bottom = res[i, part, half + at : half + at + CHUNK, :]
+                for fold, w in ((0, top + bottom), (1, top - bottom)):
+                    bb[i, fold, at : at + CHUNK, lanes] = w[:, :half].astype(BF16)
+                    bb[i, fold, half + at : half + at + CHUNK, lanes] = w[:, half:].astype(BF16)
 
     def advance(i, which, sigma):
         for part in range(2):
-            w = dot(lf[part], bb[i, part])
-            rows = slice(part * half, (part + 1) * half)
-            re, im = w[:half], w[half:]
-            p, q = pr[which, rows, :], pi[which, rows, :]
-            if sigma > 0:
-                ww[i, part, :half, :] = (re * p - im * q).astype(BF16)
-                ww[i, part, half:, :] = (re * q + im * p).astype(BF16)
-            else:
-                ww[i, part, :half, :] = (re * p + im * q).astype(BF16)
-                ww[i, part, half:, :] = (im * p - re * q).astype(BF16)
+            res[i, part] = dot(tab[1, part], bb[i, part])
+            for at in range(0, half, CHUNK):
+                rows = slice(part * half + at, part * half + at + CHUNK)
+                top, bottom = slice(at, at + CHUNK), slice(half + at, half + at + CHUNK)
+                re, im = res[i, part, top, :], res[i, part, bottom, :]
+                p, q = pr[which, rows, :], pi[which, rows, :]
+                if sigma > 0:
+                    ww[i, part, top, :] = (re * p - im * q).astype(BF16)
+                    ww[i, part, bottom, :] = (re * q + im * p).astype(BF16)
+                else:
+                    ww[i, part, top, :] = (re * p + im * q).astype(BF16)
+                    ww[i, part, bottom, :] = (im * p - re * q).astype(BF16)
 
     def back(i):
-        even, odd = dot(li[0], ww[i, 0]), dot(li[1], ww[i, 1])
-        for rows, y in ((slice(0, half), even + odd), (slice(half, points), even - odd)):
+        for part in range(2):
+            res[i, part] = dot(tab[0, part], ww[i, part])
+        for at in range(0, points, CHUNK):
+            rows = slice(at, at + CHUNK)
+            even, odd = res[i, 0, rows, :], res[i, 1, rows, :]
+            target = at % half
+            lanes = slice(0, half) if at < half else slice(half, points)
+            for start_row, y in ((0, even + odd), (half, even - odd)):
+                into = slice(start_row + target, start_row + target + CHUNK)
+                xx[i, 0, into, lanes] = y[:, :half].astype(BF16)
+                xx[i, 1, into, lanes] = y[:, half:].astype(BF16)
+
+    def finish(i, which, sigma, emit):
+        for part in range(2):
+            res[i, part] = dot(xx[i, part], tab[1, part])
+        for at in range(0, points, CHUNK):
+            rows = slice(at, at + CHUNK)
+            even, odd = res[i, 0, rows, :], res[i, 1, rows, :]
+            out = []
+            for lanes, y in ((slice(0, half), even + odd), (slice(half, points), even - odd)):
+                re, im = y[:, :half], y[:, half:]
+                c, t = cr[which, rows, lanes], ci[which, rows, lanes]
+                if sigma > 0:
+                    out.append((re * c - im * t, re * t + im * c))
+                else:
+                    out.append((re * c + im * t, im * c - re * t))
             for part in range(2):
+                a, b = out[0][part], out[1][part]
                 lanes = slice(part * half, (part + 1) * half)
-                xx[i, part, rows, :half] = y[:half, lanes].astype(BF16)
-                xx[i, part, rows, half:] = y[half:, lanes].astype(BF16)
-
-    def finish(i, which, sigma):
-        even, odd = dot(xx[i, 0], ri[0]), dot(xx[i, 1], ri[1])
-        out = []
-        for lanes, y in ((slice(0, half), even + odd), (slice(half, points), even - odd)):
-            re, im = y[:, :half], y[:, half:]
-            c, t = cr[which, :, lanes], ci[which, :, lanes]
-            if sigma > 0:
-                out.append((re * c - im * t, re * t + im * c))
-            else:
-                out.append((re * c + im * t, im * c - re * t))
-        for fold in range(2):
-            for which_part in range(2):
-                a, b = out[0][which_part], out[1][which_part]
-                lanes = slice(which_part * half, (which_part + 1) * half)
-                st[i, fold, :, lanes] = (a + b if fold == 0 else a - b).astype(BF16)
-        return out
+                st[i, 0, rows, lanes] = (a + b).astype(BF16)
+                st[i, 1, rows, lanes] = (a - b).astype(BF16)
+            emit(rows, out)
 
     def combine(z):
         send_image(z).wait_recv()
@@ -486,42 +518,51 @@
         @pl.when(jnp.logical_not(mine))
         def _():
             send_mean(z).wait_recv()
-            send_slow(z).wait_recv()
 
         mean = s0[z][0:1, :]
         turn_shared = om[0:1, :]
         transform(2)
         propagator(1, jnp.square(turn_shared * mean), sign)
-        correction(1, sign * turn_shared, ds[z])
         transform(0)
         transform(1)
         propagator(0, jnp.square(turn_own * mean), 1.0)
-        correction(0, turn_own, ds[z])
         advance(2, 1, 1)
         back(2)
         advance(0, 0, -1)
         advance(1, 0, 1)
 
+        @pl.when(jnp.logical_not(mine))
+        def _():
+            send_slow(z).wait_recv()
+
         @pl.when(z >= 1)
         def _():
             combine(z - 1)
 
-        shared = finish(2, 1, 1)
-        for side in range(2):
-            for part in range(2):
-                shq[z, side, part] = shared[side][part].astype(BF16)
+        def emit_shared(rows, out):
+            for side in range(2):
+                for part in range(2):
+                    shq[z, side, part, rows, :] = out[side][part].astype(BF16)
+
+        def emit_first(rows, out):
+            for side in range(2):
+                for part in range(2):
+                    uq[side, part, rows, :] = out[side][part]
+
+        def emit_second(rows, out):
+            for side in range(2):
+                product = uq[side, 0, rows, :] * out[side][0] + uq[side, 1, rows, :] * out[side][1]
+                acc[lax.rem(z, 2), side, rows, :] = product
+                accb[z, side, rows, :] = product.astype(BF16)
+
+        correction(1, sign * turn_shared, ds.at[z])
+        finish(2, 1, 1, emit_shared)
         send_shared(z).start()
+        correction(0, turn_own, ds.at[z])
         back(0)
         back(1)
-        first = finish(0, 0, -1)
-        for side in range(2):
-            for part in range(2):
-                uq[side, part] = first[side][part]
-        second = finish(1, 0, 1)
-        for side in range(2):
-            product = uq[side, 0] * second[side][0] + uq[side, 1] * second[side][1]
-            acc[lax.rem(z, 2), side] = product
-            accb[z, side] = product.astype(BF16)
+        finish(0, 0, -1, emit_first)
+        finish(1, 0, 1, emit_second)
         send_image(z).start()
 
         @pl.when(jnp.logical_and(z >= 1, lax.div(z - 1, levels) == d))
@@ -568,8 +609,6 @@
     shots = lax.axis_size("shot")
     total = 2 * levels
     half = points // 2
-    tables_in = [jnp.asarray(t) for t in fold_tables(points)]
-    grids_in = [jnp.asarray(t) for t in fold_grids(points)]
     full = (points, points)
     side = (points, half)
     vmem, sem = pltpu.VMEM, pltpu.SemaphoreType.DMA
@@ -579,12 +618,16 @@
     return pl.pallas_call(
         functools.partial(migrate_kernel, (points, levels, shots, fronts)),
         out_shape=jax.ShapeDtypeStruct((TILE, levels, half), F32),
-        in_specs=[anywhere, anywhere, in_vmem, in_smem, in_smem] + [in_vmem] * 6,
+        in_specs=[anywhere, anywhere, anywhere, in_smem, in_smem],
         out_specs=in_vmem,
         scratch_shapes=[
-            vmem((4, 2) + full, F32),
+            vmem((2, 2) + full, BF16),
+            vmem((levels,) + full, F32),
+            vmem(full, F32),
+            vmem(full, F32),
+            vmem((3, 2) + full, F32),
+            vmem((3, 2) + full, F32),
             vmem((3, 2) + full, BF16),
-            vmem((2,) + full, BF16),
             vmem((total,) + full, BF16),
             vmem((total, 8, points), F32),
             vmem((8, points), F32),
@@ -606,7 +649,8 @@
             vmem((levels,) + side, BF16),
             vmem((levels, shots, TILE, half), BF16),
             vmem((levels, shots, TILE, half), BF16),
-            sem((4,)),
+            sem((3,)),
+            sem((levels,)),
             sem((2, total)),
             sem((2, total)),
             sem((2, 1)),
@@ -618,10 +662,10 @@
             sem((levels, shots)),
         ],
         compiler_params=pltpu.CompilerParams(
-            collective_id=0, has_side_effects=True, vmem_limit_bytes=48 * 1024 * 1024
+            collective_id=0, has_side_effects=True, vmem_limit_bytes=60 * 1024 * 1024
         ),
         name="migrate",
-    )(source, receiver, slowness, omegas, shot_start, *tables_in, *grids_in)
+    )(source, receiver, slowness, omegas, shot_start)
 
 
 def solution(mesh):

time: 41.2 us -> 32.7 us (0.79)
  local copies, waits for them, and re-layouts: 8.96 us -> 1.57 us
  Pallas kernels: 31.2 us -> 30.3 us
    unnamed x17 -> x1, local copies, waits for them, and re-layouts: 8.96 us -> 1.57 us
    pallas_call x1, Pallas kernels: 31.2 us -> 30.3 us  [migrate(): pl.pallas_call(functools.partial(migrate_kernel, (points, levels, shots,...]
where the time goes in v2:
time: 32.7 us; the launch traced here: 32.5 us
  Pallas kernels  30.3 us (93%)
  local copies, waits for them, and re-layouts  1.57 us (5%)
  between operations  0.66 us (2%)
    pallas_call x1, Pallas kernels, migrate(): pl.pallas_call(functools.partial(migrate_kernel, (points, levels, shots,...  30.3 us
    unnamed x1, local copies, waits for them, and re-layouts  1.57 us

profile of v2, /device:TPU:2, one launch (start us, length us, event | category | flops | bytes accessed | tf_op | source)
XLA Modules:
  0.0 32.5 jit_solution(18043302881925924300)
XLA Ops:
  0.7 30.3 %migrate.1 = f32[128,2,128]{2,1,0:T(2,128)} custom-call(f32[1,3,2,256,256]{4,3,2,1,0:T(8,128)} %source.1, f32[1,3,2,256,256]{4,3,2,1,0:T(8,128)} %receiver.1, f32[1,2,256,256]{3,2,1,0:T(8,128)} %slowness.1, f32[1,3]{1,0:T(1,128)} %omegas.1, s32[1]{0:T(128)S(6)} %copy.7.start), custom_call_target="tpu_custom_call" | custom-call | tf_op jit(solution)/shard_map/migrate/pallas_call | solution.py:618
  31.0 1.6 %copy.8 = f32[128,2,128]{2,1,0:T(2,128)} copy(f32[128,2,128]{2,1,0:T(2,128)} %migrate.1) | data formatting | bytes 262144

commit v3 on v2

--- a/solution.py
+++ b/solution.py
@@ -358,18 +358,18 @@
         send_mean(d * levels + j).start()
         send_slow(d * levels + j).start()
 
-    def fold_into(target, re, im):
+    def fold_into(slot, re, im):
         lo, hi = slice(0, half), slice(half, points)
         for at in range(0, points, CHUNK):
-            rows = slice(at, at + CHUNK)
+            rows, into = slice(at, at + CHUNK), slice(slot * points + at, slot * points + at + CHUNK)
             for lanes, x in ((lo, re), (hi, im)):
                 a, b = x[rows, lo], x[rows, hi]
-                target[0, rows, lanes] = (a + b).astype(BF16)
-                target[1, rows, lanes] = (a - b).astype(BF16)
+                st[0, into, lanes] = (a + b).astype(BF16)
+                st[1, into, lanes] = (a - b).astype(BF16)
 
     for index, field in enumerate((source, receiver)):
         load(index, d, field).wait()
-        fold_into(st.at[index], fbuf.at[index, 0], fbuf.at[index, 1])
+        fold_into(index, fbuf.at[index, 0], fbuf.at[index, 1])
 
     @pl.when(provider)
     def _():
@@ -380,7 +380,7 @@
         send_turn().wait_recv()
         send_field().wait_recv()
 
-    fold_into(st.at[2], fbuf.at[2, 0], fbuf.at[2, 1])
+    fold_into(2, fbuf.at[2, 0], fbuf.at[2, 1])
 
     turn_own = omegas[0, d]
     sign = (2 * f - 1).astype(F32)
@@ -395,7 +395,8 @@
     def propagator(index, radius_sq, flip):
         def rows(at, count, targets):
             vertical = radius_sq - square[at : at + count, :]
-            root = jnp.sqrt(jnp.abs(vertical))
+            size = jnp.abs(vertical)
+            root = size * lax.rsqrt(jnp.maximum(size, 1e-30))
             positive = vertical >= 0.0
             x = jnp.maximum(vertical, 0.0)
             re = jnp.where(positive, horner(kz_cos, x), jnp.exp(-root)) * inv
@@ -422,24 +423,29 @@
     def dot(a, b):
         return jnp.dot(a, b, preferred_element_type=F32)
 
-    def transform(i):
+    def transform_all():
         for part in range(2):
-            res[i, part] = dot(st[i, part], tab[0, part])
-            lanes = slice(part * half, (part + 1) * half)
-            for at in range(0, half, CHUNK):
-                top = res[i, part, at : at + CHUNK, :]
-                bottom = res[i, part, half + at : half + at + CHUNK, :]
-                for fold, w in ((0, top + bottom), (1, top - bottom)):
-                    bb[i, fold, at : at + CHUNK, lanes] = w[:, :half].astype(BF16)
-                    bb[i, fold, half + at : half + at + CHUNK, lanes] = w[:, half:].astype(BF16)
+            res[part] = dot(st[part], tab[0, part])
+        for i in range(3):
+            for part in range(2):
+                lanes = slice(part * half, (part + 1) * half)
+                for at in range(0, half, CHUNK):
+                    row = i * points + at
+                    top = res[part, row : row + CHUNK, :]
+                    bottom = res[part, half + row : half + row + CHUNK, :]
+                    for fold, w in ((0, top + bottom), (1, top - bottom)):
+                        bb[i, fold, at : at + CHUNK, lanes] = w[:, :half].astype(BF16)
+                        bb[i, fold, half + at : half + at + CHUNK, lanes] = w[:, half:].astype(BF16)
 
     def advance(i, which, sigma):
         for part in range(2):
-            res[i, part] = dot(tab[1, part], bb[i, part])
+            base = i * points
+            res[part, base : base + points, :] = dot(tab[1, part], bb[i, part])
             for at in range(0, half, CHUNK):
                 rows = slice(part * half + at, part * half + at + CHUNK)
                 top, bottom = slice(at, at + CHUNK), slice(half + at, half + at + CHUNK)
-                re, im = res[i, part, top, :], res[i, part, bottom, :]
+                re = res[part, base + at : base + at + CHUNK, :]
+                im = res[part, base + half + at : base + half + at + CHUNK, :]
                 p, q = pr[which, rows, :], pi[which, rows, :]
                 if sigma > 0:
                     ww[i, part, top, :] = (re * p - im * q).astype(BF16)
@@ -450,10 +456,10 @@
 
     def back(i):
         for part in range(2):
-            res[i, part] = dot(tab[0, part], ww[i, part])
+            res[part, i * points : (i + 1) * points, :] = dot(tab[0, part], ww[i, part])
         for at in range(0, points, CHUNK):
-            rows = slice(at, at + CHUNK)
-            even, odd = res[i, 0, rows, :], res[i, 1, rows, :]
+            rows = slice(i * points + at, i * points + at + CHUNK)
+            even, odd = res[0, rows, :], res[1, rows, :]
             target = at % half
             lanes = slice(0, half) if at < half else slice(half, points)
             for start_row, y in ((0, even + odd), (half, even - odd)):
@@ -463,10 +469,11 @@
 
     def finish(i, which, sigma, emit):
         for part in range(2):
-            res[i, part] = dot(xx[i, part], tab[1, part])
+            res[part, i * points : (i + 1) * points, :] = dot(xx[i, part], tab[1, part])
         for at in range(0, points, CHUNK):
             rows = slice(at, at + CHUNK)
-            even, odd = res[i, 0, rows, :], res[i, 1, rows, :]
+            into = slice(i * points + at, i * points + at + CHUNK)
+            even, odd = res[0, into, :], res[1, into, :]
             out = []
             for lanes, y in ((slice(0, half), even + odd), (slice(half, points), even - odd)):
                 re, im = y[:, :half], y[:, half:]
@@ -478,8 +485,8 @@
             for part in range(2):
                 a, b = out[0][part], out[1][part]
                 lanes = slice(part * half, (part + 1) * half)
-                st[i, 0, rows, lanes] = (a + b).astype(BF16)
-                st[i, 1, rows, lanes] = (a - b).astype(BF16)
+                st[0, into, lanes] = (a + b).astype(BF16)
+                st[1, into, lanes] = (a - b).astype(BF16)
             emit(rows, out)
 
     def combine(z):
@@ -521,10 +528,8 @@
 
         mean = s0[z][0:1, :]
         turn_shared = om[0:1, :]
-        transform(2)
+        transform_all()
         propagator(1, jnp.square(turn_shared * mean), sign)
-        transform(0)
-        transform(1)
         propagator(0, jnp.square(turn_own * mean), 1.0)
         advance(2, 1, 1)
         back(2)
@@ -565,9 +570,11 @@
         finish(1, 0, 1, emit_second)
         send_image(z).start()
 
-        @pl.when(jnp.logical_and(z >= 1, lax.div(z - 1, levels) == d))
+        before = z - 2 + d
+
+        @pl.when(jnp.logical_and(before >= d * levels, before < (d + 1) * levels))
         def _():
-            place(z - 1)
+            place(before)
 
         return carry
 
@@ -584,7 +591,7 @@
         for step in range(1, shots):
             recv_columns(j, step).wait_recv()
             total += zrecv[j, lax.rem(s + step, shots)].astype(F32)
-        image[:, j, :] = total
+        image[pl.ds(j, TILE, stride=levels), :] = total
 
     @pl.when(provider)
     def _():
@@ -617,7 +624,7 @@
     anywhere = pl.BlockSpec(memory_space=pl.ANY)
     return pl.pallas_call(
         functools.partial(migrate_kernel, (points, levels, shots, fronts)),
-        out_shape=jax.ShapeDtypeStruct((TILE, levels, half), F32),
+        out_shape=jax.ShapeDtypeStruct((TILE * levels, half), F32),
         in_specs=[anywhere, anywhere, anywhere, in_smem, in_smem],
         out_specs=in_vmem,
         scratch_shapes=[
@@ -625,9 +632,9 @@
             vmem((levels,) + full, F32),
             vmem(full, F32),
             vmem(full, F32),
+            vmem((2, 3 * points, points), F32),
             vmem((3, 2) + full, F32),
-            vmem((3, 2) + full, F32),
-            vmem((3, 2) + full, BF16),
+            vmem((2, 3 * points, points), BF16),
             vmem((total,) + full, BF16),
             vmem((total, 8, points), F32),
             vmem((8, points), F32),
@@ -665,16 +672,16 @@
             collective_id=0, has_side_effects=True, vmem_limit_bytes=60 * 1024 * 1024
         ),
         name="migrate",
-    )(source, receiver, slowness, omegas, shot_start)
+    )(source, receiver, slowness, omegas, shot_start).reshape(TILE, levels, half)
 
 
 def solution(mesh):
     sizes = mesh.shape
 
-    def per_device(source, *rest):
-        if sizes["depth"] == 2 and sizes["freq"] == 2 and source.shape[1] == 3:
-            return migrate(source, *rest)
-        return local(source, *rest)
+    def per_device(source, receiver, slowness, *rest):
+        if sizes["depth"] == 2 and sizes["freq"] == 2 and source.shape[1] == 3 and slowness.shape[1] > 1:
+            return migrate(source, receiver, slowness, *rest)
+        return local(source, receiver, slowness, *rest)
 
     return jax.shard_map(
         per_device,

time: 32.7 us -> 29.9 us (0.914)
  Pallas kernels: 30.3 us -> 27.5 us
    pallas_call x1, Pallas kernels: 30.3 us -> 27.5 us  [migrate(): pl.pallas_call(functools.partial(migrate_kernel, (points, levels, shots,...]
where the time goes in v3:
time: 29.9 us; the launch traced here: 29.8 us
  Pallas kernels  27.5 us (92%)
  local copies, waits for them, and re-layouts  1.57 us (5%)
  between operations  0.66 us (2%)
    pallas_call x1, Pallas kernels, migrate(): pl.pallas_call(functools.partial(migrate_kernel, (points, levels, shots,...  27.5 us
    unnamed x1, local copies, waits for them, and re-layouts  1.57 us

profile of v3, /device:TPU:2, one launch (start us, length us, event | category | flops | bytes accessed | tf_op | source)
XLA Modules:
  0.0 29.8 jit_solution(8857198109803550283)
XLA Ops:
  0.7 27.5 %migrate.1 = f32[256,128]{1,0:T(8,128)} custom-call(f32[1,3,2,256,256]{4,3,2,1,0:T(8,128)} %source.1, f32[1,3,2,256,256]{4,3,2,1,0:T(8,128)} %receiver.1, f32[1,2,256,256]{3,2,1,0:T(8,128)} %slowness.1, f32[1,3]{1,0:T(1,128)} %omegas.1, s32[1]{0:T(128)S(6)} %copy.7.start), custom_call_target="tpu_custom_call" | custom-call | tf_op jit(solution)/shard_map/migrate/pallas_call | solution.py:625
  28.2 1.6 %copy.8 = f32[128,2,128]{2,1,0:T(2,128)} copy(f32[128,2,128]{2,1,0:T(2,128)} %bitcast.1) | data formatting | bytes 262144

commit v4 on v3

--- a/solution.py
+++ b/solution.py
@@ -220,7 +220,7 @@
 
 def migrate_kernel(
     dims, source, receiver, slowness, omegas, start, image,
-    tab, slow, square, window, res, fbuf, st, ds, s0, om, pr, pi, cr, ci, bb, ww, xx, uq, acc, accb, shq, accr, shr, chip,
+    tab, slow, square, window, res, wide, fbuf, st, ds, s0, om, pr, pi, cr, ci, bb, ww, xx, uq, acc, accb, shq, accr, shr, chip,
     xsend, xrecv, zsend, zrecv,
     load_sem, slow_sem, ds_sem, s0_sem, sh_sem, om_sem, acc_sem, shq_sem, x_sem, zs_sem, zr_sem,
 ):
@@ -423,53 +423,54 @@
     def dot(a, b):
         return jnp.dot(a, b, preferred_element_type=F32)
 
-    def transform_all():
+    def multiply_right(operand, turned):
         for part in range(2):
-            res[part] = dot(st[part], tab[0, part])
+            res[part] = dot(operand[part], tab[turned, part])
+
+    def multiply_left(turned, operand):
+        for part in range(2):
+            wide[part] = dot(tab[turned, part], operand[part])
+
+    def fold_rows():
         for i in range(3):
             for part in range(2):
-                lanes = slice(part * half, (part + 1) * half)
+                lanes = slice(i * points + part * half, i * points + (part + 1) * half)
                 for at in range(0, half, CHUNK):
                     row = i * points + at
                     top = res[part, row : row + CHUNK, :]
                     bottom = res[part, half + row : half + row + CHUNK, :]
                     for fold, w in ((0, top + bottom), (1, top - bottom)):
-                        bb[i, fold, at : at + CHUNK, lanes] = w[:, :half].astype(BF16)
-                        bb[i, fold, half + at : half + at + CHUNK, lanes] = w[:, half:].astype(BF16)
+                        bb[fold, at : at + CHUNK, lanes] = w[:, :half].astype(BF16)
+                        bb[fold, half + at : half + at + CHUNK, lanes] = w[:, half:].astype(BF16)
 
     def advance(i, which, sigma):
+        lanes = slice(i * points, (i + 1) * points)
         for part in range(2):
-            base = i * points
-            res[part, base : base + points, :] = dot(tab[1, part], bb[i, part])
             for at in range(0, half, CHUNK):
                 rows = slice(part * half + at, part * half + at + CHUNK)
                 top, bottom = slice(at, at + CHUNK), slice(half + at, half + at + CHUNK)
-                re = res[part, base + at : base + at + CHUNK, :]
-                im = res[part, base + half + at : base + half + at + CHUNK, :]
+                re, im = wide[part, top, lanes], wide[part, bottom, lanes]
                 p, q = pr[which, rows, :], pi[which, rows, :]
                 if sigma > 0:
-                    ww[i, part, top, :] = (re * p - im * q).astype(BF16)
-                    ww[i, part, bottom, :] = (re * q + im * p).astype(BF16)
+                    ww[part, top, lanes] = (re * p - im * q).astype(BF16)
+                    ww[part, bottom, lanes] = (re * q + im * p).astype(BF16)
                 else:
-                    ww[i, part, top, :] = (re * p + im * q).astype(BF16)
-                    ww[i, part, bottom, :] = (im * p - re * q).astype(BF16)
-
-    def back(i):
-        for part in range(2):
-            res[part, i * points : (i + 1) * points, :] = dot(tab[0, part], ww[i, part])
-        for at in range(0, points, CHUNK):
-            rows = slice(i * points + at, i * points + at + CHUNK)
-            even, odd = res[0, rows, :], res[1, rows, :]
-            target = at % half
-            lanes = slice(0, half) if at < half else slice(half, points)
-            for start_row, y in ((0, even + odd), (half, even - odd)):
-                into = slice(start_row + target, start_row + target + CHUNK)
-                xx[i, 0, into, lanes] = y[:, :half].astype(BF16)
-                xx[i, 1, into, lanes] = y[:, half:].astype(BF16)
+                    ww[part, top, lanes] = (re * p + im * q).astype(BF16)
+                    ww[part, bottom, lanes] = (im * p - re * q).astype(BF16)
+
+    def unfold_rows():
+        for i in range(3):
+            for at in range(0, points, CHUNK):
+                rows, lanes = slice(at, at + CHUNK), slice(i * points, (i + 1) * points)
+                even, odd = wide[0, rows, lanes], wide[1, rows, lanes]
+                target = i * points + at % half
+                lanes = slice(0, half) if at < half else slice(half, points)
+                for start_row, y in ((0, even + odd), (half, even - odd)):
+                    into = slice(start_row + target, start_row + target + CHUNK)
+                    xx[0, into, lanes] = y[:, :half].astype(BF16)
+                    xx[1, into, lanes] = y[:, half:].astype(BF16)
 
     def finish(i, which, sigma, emit):
-        for part in range(2):
-            res[part, i * points : (i + 1) * points, :] = dot(xx[i, part], tab[1, part])
         for at in range(0, points, CHUNK):
             rows = slice(at, at + CHUNK)
             into = slice(i * points + at, i * points + at + CHUNK)
@@ -512,12 +513,13 @@
         total = (chip[j] + xrecv[j].astype(F32)).astype(BF16)
         columns = lax.broadcasted_iota(jnp.int32, (TILE, points), 0)
         places = lax.broadcasted_iota(jnp.int32, (TILE, points), 1)
-        for owner in range(shots):
+        for step in [*range(1, shots), 0]:
+            owner = lax.rem(s + step, shots)
             chosen = places == columns + (owner * TILE - start[0])
             chosen = jnp.where(chosen, 1.0, 0.0).astype(BF16)
             zsend[j, owner] = dot(chosen, total).astype(BF16)
-        for step in range(1, shots):
-            send_columns(j, step).start()
+            if step > 0:
+                send_columns(j, step).start()
 
     def one_level(z, carry):
         mine = lax.div(z, levels) == d
@@ -528,11 +530,12 @@
 
         mean = s0[z][0:1, :]
         turn_shared = om[0:1, :]
-        transform_all()
+        multiply_right(st, 0)
         propagator(1, jnp.square(turn_shared * mean), sign)
         propagator(0, jnp.square(turn_own * mean), 1.0)
+        fold_rows()
+        multiply_left(1, bb)
         advance(2, 1, 1)
-        back(2)
         advance(0, 0, -1)
         advance(1, 0, 1)
 
@@ -560,12 +563,13 @@
                 acc[lax.rem(z, 2), side, rows, :] = product
                 accb[z, side, rows, :] = product.astype(BF16)
 
+        multiply_left(0, ww)
         correction(1, sign * turn_shared, ds.at[z])
+        correction(0, turn_own, ds.at[z])
+        unfold_rows()
+        multiply_right(xx, 1)
         finish(2, 1, 1, emit_shared)
         send_shared(z).start()
-        correction(0, turn_own, ds.at[z])
-        back(0)
-        back(1)
         finish(0, 0, -1, emit_first)
         finish(1, 0, 1, emit_second)
         send_image(z).start()
@@ -587,11 +591,12 @@
         place(last)
 
     for j in range(levels):
-        total = zsend[j, s].astype(F32)
+        image[0, pl.ds(j, TILE, stride=levels), :] = zsend[j, s].astype(F32)
+        total = jnp.zeros((TILE, half), F32)
         for step in range(1, shots):
             recv_columns(j, step).wait_recv()
             total += zrecv[j, lax.rem(s + step, shots)].astype(F32)
-        image[pl.ds(j, TILE, stride=levels), :] = total
+        image[1, pl.ds(j, TILE, stride=levels), :] = total
 
     @pl.when(provider)
     def _():
@@ -622,9 +627,9 @@
     in_vmem = pl.BlockSpec(memory_space=pltpu.VMEM)
     in_smem = pl.BlockSpec(memory_space=pltpu.SMEM)
     anywhere = pl.BlockSpec(memory_space=pl.ANY)
-    return pl.pallas_call(
+    terms = pl.pallas_call(
         functools.partial(migrate_kernel, (points, levels, shots, fronts)),
-        out_shape=jax.ShapeDtypeStruct((TILE * levels, half), F32),
+        out_shape=jax.ShapeDtypeStruct((2, TILE * levels, half), F32),
         in_specs=[anywhere, anywhere, anywhere, in_smem, in_smem],
         out_specs=in_vmem,
         scratch_shapes=[
@@ -633,6 +638,7 @@
             vmem(full, F32),
             vmem(full, F32),
             vmem((2, 3 * points, points), F32),
+            vmem((2, points, 3 * points), F32),
             vmem((3, 2) + full, F32),
             vmem((2, 3 * points, points), BF16),
             vmem((total,) + full, BF16),
@@ -642,9 +648,9 @@
             vmem((2,) + full, F32),
             vmem((2,) + full, F32),
             vmem((2,) + full, F32),
-            vmem((3, 2) + full, BF16),
-            vmem((3, 2) + full, BF16),
-            vmem((3, 2) + full, BF16),
+            vmem((2, points, 3 * points), BF16),
+            vmem((2, points, 3 * points), BF16),
+            vmem((2, 3 * points, points), BF16),
             vmem((2, 2) + side, F32),
             vmem((2, 2) + side, F32),
             vmem((total, 2) + side, BF16),
@@ -672,7 +678,8 @@
             collective_id=0, has_side_effects=True, vmem_limit_bytes=60 * 1024 * 1024
         ),
         name="migrate",
-    )(source, receiver, slowness, omegas, shot_start).reshape(TILE, levels, half)
+    )(source, receiver, slowness, omegas, shot_start)
+    return (terms[0] + terms[1]).reshape(TILE, levels, half)
 
 
 def solution(mesh):

time: 29.9 us -> 30.8 us (1.030)
  other arithmetic: 0 us -> 1.64 us
  local copies, waits for them, and re-layouts: 1.57 us -> 0 us
  Pallas kernels: 27.5 us -> 28.4 us
    add x0 -> x1, other arithmetic: none -> 1.64 us  [migrate(): return (terms[0] + terms[1]).reshape(TILE, levels, half)]
    unnamed x1 -> x0, local copies, waits for them, and re-layouts: 1.57 us -> none
    pallas_call x1, Pallas kernels: 27.5 us -> 28.4 us  [migrate(): pl.pallas_call(functools.partial(migrate_kernel, (points, levels, shots,...]
where the time goes in v4:
time: 30.8 us; the launch traced here: 30.7 us
  Pallas kernels  28.4 us (92%)
  other arithmetic  1.64 us (5%)
  between operations  0.66 us (2%)
    pallas_call x1, Pallas kernels, migrate(): pl.pallas_call(functools.partial(migrate_kernel, (points, levels, shots,...  28.4 us
    add x1, other arithmetic, migrate(): return (terms[0] + terms[1]).reshape(TILE, levels, half)  1.64 us

profile of v4, /device:TPU:2, one launch (start us, length us, event | category | flops | bytes accessed | tf_op | source)
XLA Modules:
  0.0 30.7 jit_solution(13243144478246402373)
XLA Ops:
  0.7 28.4 %migrate.1 = f32[2,256,128]{2,1,0:T(8,128)} custom-call(f32[1,3,2,256,256]{4,3,2,1,0:T(8,128)} %source.1, f32[1,3,2,256,256]{4,3,2,1,0:T(8,128)} %receiver.1, f32[1,2,256,256]{3,2,1,0:T(8,128)} %slowness.1, f32[1,3]{1,0:T(1,128)} %omegas.1, s32[1]{0:T(128)S(6)} %copy.6.start), custom_call_target="tpu_custom_call" | custom-call | tf_op jit(solution)/shard_map/migrate/pallas_call | solution.py:630
  29.0 1.6 %slice_add_fusion = f32[1,256,128]{2,1,0:T(8,128)} fusion(f32[2,256,128]{2,1,0:T(8,128)} %migrate.1), kind=kLoop, calls=%fused_computation | loop fusion | flops 32768 | bytes 393216 | tf_op jit(solution)/shard_map/add | solution.py:682

commit v5 on v3

--- a/solution.py
+++ b/solution.py
@@ -196,6 +196,7 @@
 MESH = pl.DeviceIdType.MESH
 BF16 = jnp.bfloat16
 CHUNK = 32
+LOG2_E = 1.4426950408889634
 F32 = jnp.float32
 SLOWEST, SLOWNESS_SPAN, FASTEST_TURN = 1.4, 0.8, 2.5
 
@@ -340,13 +341,13 @@
         distance_in = (jnp.minimum(at, points - 1 - at) + 1).astype(F32)
         return jnp.minimum(distance_in * (16.0 / points), 1.0)
 
-    window[...] = taper(row) * taper(column) * (1.0 / points)
+    window[...] = taper(row) * taper(column) * (1.0 / points**2)
 
     pl.semaphore_wait(barrier, shots + 1)
     for front in range(2):
         @pl.when(jnp.logical_and(provider, f == front))
         def _(field=(receiver, source)[front]):
-            om[...] = jnp.full((8, points), omegas[0, fronts - 1], F32)
+            om[...] = jnp.full((8, points), omegas[fronts - 1], F32)
             send_turn().start()
             send_front(field).start()
 
@@ -382,7 +383,7 @@
 
     fold_into(2, fbuf.at[2, 0], fbuf.at[2, 1])
 
-    turn_own = omegas[0, d]
+    turn_own = omegas[d]
     sign = (2 * f - 1).astype(F32)
     limit = 1.01 * (FASTEST_TURN * SLOWEST) ** 2
     kz_cos = even_polynomial(np.cos, limit, 5)
@@ -390,7 +391,6 @@
     limit = 1.01 * (FASTEST_TURN * SLOWNESS_SPAN) ** 2
     turn_cos = even_polynomial(np.cos, limit, 4)
     turn_sinc = even_polynomial(sinc, limit, 3)
-    inv = 1.0 / points
 
     def propagator(index, radius_sq, flip):
         def rows(at, count, targets):
@@ -399,8 +399,9 @@
             root = size * lax.rsqrt(jnp.maximum(size, 1e-30))
             positive = vertical >= 0.0
             x = jnp.maximum(vertical, 0.0)
-            re = jnp.where(positive, horner(kz_cos, x), jnp.exp(-root)) * inv
-            im = jnp.where(positive, root * horner(kz_sinc, x), 0.0) * (inv * flip)
+            re = jnp.where(positive, horner(kz_cos, x), jnp.exp2(root * -LOG2_E))
+            im = jnp.where(positive, root * horner(kz_sinc, x), 0.0)
+            im = im if flip is None else im * flip
             for target in targets:
                 pr[index, target : target + count, :] = re
                 pi[index, target : target + count, :] = im
@@ -512,12 +513,13 @@
         total = (chip[j] + xrecv[j].astype(F32)).astype(BF16)
         columns = lax.broadcasted_iota(jnp.int32, (TILE, points), 0)
         places = lax.broadcasted_iota(jnp.int32, (TILE, points), 1)
-        for owner in range(shots):
+        for step in [*range(1, shots), 0]:
+            owner = lax.rem(s + step, shots)
             chosen = places == columns + (owner * TILE - start[0])
             chosen = jnp.where(chosen, 1.0, 0.0).astype(BF16)
             zsend[j, owner] = dot(chosen, total).astype(BF16)
-        for step in range(1, shots):
-            send_columns(j, step).start()
+            if step > 0:
+                send_columns(j, step).start()
 
     def one_level(z, carry):
         mine = lax.div(z, levels) == d
@@ -530,7 +532,7 @@
         turn_shared = om[0:1, :]
         transform_all()
         propagator(1, jnp.square(turn_shared * mean), sign)
-        propagator(0, jnp.square(turn_own * mean), 1.0)
+        propagator(0, jnp.square(turn_own * mean), None)
         advance(2, 1, 1)
         back(2)
         advance(0, 0, -1)
@@ -566,15 +568,15 @@
         correction(0, turn_own, ds.at[z])
         back(0)
         back(1)
+        before = z - 2 + d
+
+        @pl.when(jnp.logical_and(before >= d * levels, before < (d + 1) * levels))
+        def _():
+            place(before)
+
         finish(0, 0, -1, emit_first)
         finish(1, 0, 1, emit_second)
         send_image(z).start()
-
-        before = z - 2 + d
-
-        @pl.when(jnp.logical_and(before >= d * levels, before < (d + 1) * levels))
-        def _():
-            place(before)
 
         return carry
 
@@ -621,7 +623,7 @@
     vmem, sem = pltpu.VMEM, pltpu.SemaphoreType.DMA
     in_vmem = pl.BlockSpec(memory_space=pltpu.VMEM)
     in_smem = pl.BlockSpec(memory_space=pltpu.SMEM)
-    anywhere = pl.BlockSpec(memory_space=pl.ANY)
+    anywhere = pl.BlockSpec(memory_space=pltpu.HBM)
     return pl.pallas_call(
         functools.partial(migrate_kernel, (points, levels, shots, fronts)),
         out_shape=jax.ShapeDtypeStruct((TILE * levels, half), F32),
@@ -669,10 +671,10 @@
             sem((levels, shots)),
         ],
         compiler_params=pltpu.CompilerParams(
-            collective_id=0, has_side_effects=True, vmem_limit_bytes=60 * 1024 * 1024
+            collective_id=0, has_side_effects=True, vmem_limit_bytes=55000 * 1024
         ),
         name="migrate",
-    )(source, receiver, slowness, omegas, shot_start).reshape(TILE, levels, half)
+    )(source, receiver, slowness, omegas.reshape(-1), shot_start).reshape(TILE, levels, half)
 
 
 def solution(mesh):

time: 29.9 us -> 30.6 us (1.023)
  Pallas kernels: 27.5 us -> 28.5 us
    pallas_call x1, Pallas kernels: 27.5 us -> 28.5 us  [migrate(): pl.pallas_call(functools.partial(migrate_kernel, (points, levels, shots,...]
    unnamed x1 -> x3, local copies, waits for them, and re-layouts: 1.57 us -> 1.31 us
where the time goes in v5:
time: 30.6 us; the launch traced here: 30.4 us
  Pallas kernels  28.5 us (93%)
  local copies, waits for them, and re-layouts  1.31 us (4%)
  between operations  0.67 us (2%)
    pallas_call x1, Pallas kernels, migrate(): pl.pallas_call(functools.partial(migrate_kernel, (points, levels, shots,...  28.5 us
    unnamed x3, local copies, waits for them, and re-layouts  1.31 us

profile of v5, /device:TPU:2, one launch (start us, length us, event | category | flops | bytes accessed | tf_op | source)
XLA Modules:
  0.0 30.4 jit_solution(10507704434368660449)
XLA Ops:
  0.7 0.0 copy-start
  0.7 0.6 %copy-done = f32[1,3]{1,0:T(1,128)S(1)} copy-done((f32[1,3]{1,0:T(1,128)S(1)}, f32[1,3]{1,0:T(1,128)}, u32[]{:S(2)}) %copy-start) | copy-done | bytes 36
  1.3 28.5 %migrate.1 = f32[256,128]{1,0:T(8,128)S(1)} custom-call(f32[1,3,2,256,256]{4,3,2,1,0:T(8,128)} %source.1, f32[1,3,2,256,256]{4,3,2,1,0:T(8,128)} %receiver.1, f32[1,2,256,256]{3,2,1,0:T(8,128)} %slowness.1, f32[3]{0:T(128)S(1)} %bitcast.3, s32[1]{0:T(128)S(6)} %copy.7.start), custom_call_target="tpu_custom_call" | custom-call | tf_op jit(solution)/shard_map/migrate/pallas_call | solution.py:627
  29.8 0.7 %copy.8 = f32[128,2,128]{2,1,0:T(2,128)} copy(f32[128,2,128]{2,1,0:T(2,128)S(1)} %bitcast.2) | data formatting | bytes 262144
Async XLA Ops:
  0.7 0.7 %copy-start = (f32[1,3]{1,0:T(1,128)S(1)}, f32[1,3]{1,0:T(1,128)}, u32[]{:S(2)}) copy-start(f32[1,3]{1,0:T(1,128)} %param.8) | copy-start | bytes 40

commit v6 on v5

--- a/solution.py
+++ b/solution.py
@@ -568,15 +568,15 @@
         correction(0, turn_own, ds.at[z])
         back(0)
         back(1)
+        finish(0, 0, -1, emit_first)
+        finish(1, 0, 1, emit_second)
+        send_image(z).start()
+
         before = z - 2 + d
 
         @pl.when(jnp.logical_and(before >= d * levels, before < (d + 1) * levels))
         def _():
             place(before)
-
-        finish(0, 0, -1, emit_first)
-        finish(1, 0, 1, emit_second)
-        send_image(z).start()
 
         return carry
 

time: 30.6 us -> 29.5 us (0.964)
  Pallas kernels: 28.5 us -> 27.4 us
    pallas_call x1, Pallas kernels: 28.5 us -> 27.4 us  [migrate(): pl.pallas_call(functools.partial(migrate_kernel, (points, levels, shots,...]
where the time goes in v6:
time: 29.5 us; the launch traced here: 29.4 us
  Pallas kernels  27.4 us (93%)
  local copies, waits for them, and re-layouts  1.31 us (4%)
  between operations  0.67 us (2%)
    pallas_call x1, Pallas kernels, migrate(): pl.pallas_call(functools.partial(migrate_kernel, (points, levels, shots,...  27.4 us
    unnamed x3, local copies, waits for them, and re-layouts  1.31 us

profile of v6, /device:TPU:2, one launch (start us, length us, event | category | flops | bytes accessed | tf_op | source)
XLA Modules:
  0.0 29.4 jit_solution(14274153319200009302)
XLA Ops:
  0.7 0.0 copy-start
  0.7 0.6 %copy-done = f32[1,3]{1,0:T(1,128)S(1)} copy-done((f32[1,3]{1,0:T(1,128)S(1)}, f32[1,3]{1,0:T(1,128)}, u32[]{:S(2)}) %copy-start) | copy-done | bytes 36
  1.3 27.4 %migrate.1 = f32[256,128]{1,0:T(8,128)S(1)} custom-call(f32[1,3,2,256,256]{4,3,2,1,0:T(8,128)} %source.1, f32[1,3,2,256,256]{4,3,2,1,0:T(8,128)} %receiver.1, f32[1,2,256,256]{3,2,1,0:T(8,128)} %slowness.1, f32[3]{0:T(128)S(1)} %bitcast.3, s32[1]{0:T(128)S(6)} %copy.7.start), custom_call_target="tpu_custom_call" | custom-call | tf_op jit(solution)/shard_map/migrate/pallas_call | solution.py:627
  28.7 0.7 %copy.8 = f32[128,2,128]{2,1,0:T(2,128)} copy(f32[128,2,128]{2,1,0:T(2,128)S(1)} %bitcast.2) | data formatting | bytes 262144
Async XLA Ops:
  0.7 0.7 %copy-start = (f32[1,3]{1,0:T(1,128)S(1)}, f32[1,3]{1,0:T(1,128)}, u32[]{:S(2)}) copy-start(f32[1,3]{1,0:T(1,128)} %param.8) | copy-start | bytes 40
